TPU v7x, 32 devices: a whole 2x2x4 slice. The times are simulated.
32 devices in a mesh: seq: 4 (over y, core), ctx: 8 (over z, x).
Axes of the slice: x: 2, y: 2, z: 4, core: 2. Of those that a mesh axis runs over, the one named last changes fastest.
Arguments:
- tokens: bfloat16 [4, 1024, 2048], P('seq', 'ctx'), may hold values from -6 to 6
- positions: int32 [4, 1024], P('seq', 'ctx'), may hold values from 0 to 1022, as said below
- cotangent: bfloat16 [4, 1024, 2048], P('seq', 'ctx'), may hold values from -6 to 6
- w_query: bfloat16 [2048, 2048], P(('seq', 'ctx')), may hold values from -0.125 to 0.125
- w_key: bfloat16 [2048, 1024], P(('seq', 'ctx')), may hold values from -0.125 to 0.125
- w_value: bfloat16 [2048, 1024], P(('seq', 'ctx')), may hold values from -0.125 to 0.125
- w_out: bfloat16 [2048, 2048], P(('seq', 'ctx')), may hold values from -0.5 to 0.5
- w_gate: bfloat16 [2048, 6144], P(('seq', 'ctx')), may hold values from -0.125 to 0.125
- w_up: bfloat16 [2048, 6144], P(('seq', 'ctx')), may hold values from -0.125 to 0.125
- w_down: bfloat16 [6144, 2048], P(('seq', 'ctx')), may hold values from -0.078125 to 0.078125
- attn_gain: bfloat16 [2048], P(('seq', 'ctx')), may hold values from 0.099609375 to 1.8984375
- mlp_gain: bfloat16 [2048], P(('seq', 'ctx')), may hold values from 0.099609375 to 1.8984375
- query_gain: bfloat16 [128], P(('seq', 'ctx')), may hold values from 1 to 2.5
- key_gain: bfloat16 [128], P(('seq', 'ctx')), may hold values from 1 to 2.5
Outputs:
- block_out: bfloat16 [4, 1024, 2048], P('seq', 'ctx')
- grad_tokens: float32 [4, 1024, 2048], P('seq', 'ctx')
- grad_query: float32 [2048, 2048], P(('seq', 'ctx'))
- grad_key: float32 [2048, 1024], P(('seq', 'ctx'))
- grad_value: float32 [2048, 1024], P(('seq', 'ctx'))
- grad_out: float32 [2048, 2048], P(('seq', 'ctx'))
- grad_gate: float32 [2048, 6144], P(('seq', 'ctx'))
- grad_up: float32 [2048, 6144], P(('seq', 'ctx'))
- grad_down: float32 [6144, 2048], P(('seq', 'ctx'))
- grad_attn_gain: float32 [2048], P(('seq', 'ctx'))
- grad_mlp_gain: float32 [2048], P(('seq', 'ctx'))
- grad_query_gain: float32 [128], P(('seq', 'ctx'))
- grad_key_gain: float32 [128], P(('seq', 'ctx'))
Inputs may be any that keep to these rules, and one draw needn't show every extreme that they name: `positions`: each sequence is cut into contiguous documents, and a token's position is its index minus the index of its document's first token. In one sequence, drawn from the seed, the first document is one token long and the second fills the rest of the sequence. In every other sequence each document has from max(1, 50) to 500 tokens, drawn evenly, and only the last one may be cut shorter by the sequence's end.
All inputs are finite; a program needn't handle non-finite values.
Results may differ from a plain program's by a relative error of at most 0.017.
The roundings to bfloat16 on the way count: a program that leaves them out, or rounds other values in their place, can miss the bound.
Values may be sent and summed in bfloat16 or wider, within the bound.
No kernel may reach another device: no remote copies, remote signals or barrier semaphores. Data moves between devices by JAX's collectives and lax.ppermute only.
A program may use at most 512 MiB of HBM per device.

v0:
```python
from functools import partial

import jax
import jax.numpy as jnp
from jax import lax
from jax.sharding import PartitionSpec as P

HEADS = 16
KV_HEADS = 8
HEAD_DIM = 128


EPS = 1e-06
THETA = 1000000.0
NEG = -1e30


def root_norm(value, gain):
    return value * lax.rsqrt(jnp.mean(value * value, axis=-1, keepdims=True) + EPS) * gain


def rotate(value, where):
    half = value.shape[-1] // 2
    freq = THETA ** (-jnp.arange(half, dtype=jnp.float32) * 2.0 / value.shape[-1])
    angle = where.astype(jnp.float32)[:, None] * freq[None, :]
    cosine = jnp.cos(angle)[:, None, :]
    sine = jnp.sin(angle)[:, None, :]
    first = value[..., :half]
    second = value[..., half:]
    return jnp.concatenate(
        [first * cosine - second * sine, second * cosine + first * sine], axis=-1
    )


def head_prep(value, gain, where):
    return rotate(root_norm(value, gain), where)


def swiglu(gate, upval):
    return jax.nn.silu(gate) * upval


def product(left, right):
    return jnp.dot(left, right, preferred_element_type=jnp.float32)


def product_left(left, right):
    return lax.dot_general(
        left, right, (((0,), (0,)), ((), ())), preferred_element_type=jnp.float32
    )


def product_right(left, right):
    return lax.dot_general(
        left, right, (((1,), (1,)), ((), ())), preferred_element_type=jnp.float32
    )


def body(
    tokens,
    positions,
    cotangent,
    w_query,
    w_key,
    w_value,
    w_out,
    w_gate,
    w_up,
    w_down,
    attn_gain,
    mlp_gain,
    query_gain,
    key_gain,
):
    rows = tokens.shape[1]
    group = HEADS // KV_HEADS
    scale = HEAD_DIM ** (-0.5)
    inputs = tokens[0].astype(jnp.float32)
    where = positions[0]
    upstream = cotangent[0]
    place = lax.axis_index("ctx") * rows + jnp.arange(rows, dtype=jnp.int32)
    full_query, full_key, full_value, full_out, gain_attn, gain_query, gain_key = (
        lax.all_gather(w_query, ("seq", "ctx"), axis=0, tiled=True),
        lax.all_gather(w_key, ("seq", "ctx"), axis=0, tiled=True),
        lax.all_gather(w_value, ("seq", "ctx"), axis=0, tiled=True),
        lax.all_gather(w_out, ("seq", "ctx"), axis=0, tiled=True),
        lax.all_gather(attn_gain, ("seq", "ctx"), axis=0, tiled=True),
        lax.all_gather(query_gain, ("seq", "ctx"), axis=0, tiled=True),
        lax.all_gather(key_gain, ("seq", "ctx"), axis=0, tiled=True),
    )
    normed_one, pull_one = jax.vjp(root_norm, inputs, gain_attn.astype(jnp.float32))
    low_one = normed_one.astype(jnp.bfloat16)
    query_raw = product(low_one, full_query).reshape(rows, HEADS, HEAD_DIM)
    key_raw = product(low_one, full_key).reshape(rows, KV_HEADS, HEAD_DIM)
    value_low = product(low_one, full_value).astype(jnp.bfloat16)
    prepare = partial(head_prep, where=where)
    query_rot, pull_query = jax.vjp(prepare, query_raw, gain_query.astype(jnp.float32))
    key_rot, pull_key = jax.vjp(prepare, key_raw, gain_key.astype(jnp.float32))
    query_low = query_rot.astype(jnp.bfloat16).reshape(rows, KV_HEADS, group, HEAD_DIM)
    key_low = key_rot.astype(jnp.bfloat16).reshape(rows, KV_HEADS * HEAD_DIM)
    keys_all, values_all = (
        lax.all_gather(key_low, "ctx", axis=0, tiled=True),
        lax.all_gather(value_low, "ctx", axis=0, tiled=True),
    )
    length = keys_all.shape[0]
    keys_three = keys_all.reshape(length, KV_HEADS, HEAD_DIM)
    values_three = values_all.reshape(length, KV_HEADS, HEAD_DIM)
    spots = jnp.arange(length, dtype=jnp.int32)
    visible = (spots[None, :] <= place[:, None]) & (spots[None, :] >= (place - where)[:, None])

    def score_block():
        raw = (
            jnp.einsum("tkgd,skd->kgts", query_low, keys_three, preferred_element_type=jnp.float32)
            * scale
        )
        return jnp.where(visible[None, None], raw, NEG)

    scores = score_block()
    peak = jnp.max(scores, axis=-1, keepdims=True)
    powers = jnp.exp(scores - peak)
    totals = jnp.sum(powers, axis=-1, keepdims=True)
    share = powers / totals
    log_total = peak + jnp.log(totals)
    heads_out = jnp.einsum(
        "kgts,skd->tkgd",
        share.astype(jnp.bfloat16),
        values_three,
        preferred_element_type=jnp.float32,
    )
    heads_low = heads_out.reshape(rows, HEADS * HEAD_DIM).astype(jnp.bfloat16)
    resid = inputs + product(heads_low, full_out)
    full_gate, full_up, full_down, gain_mlp = (
        lax.all_gather(w_gate, ("seq", "ctx"), axis=0, tiled=True),
        lax.all_gather(w_up, ("seq", "ctx"), axis=0, tiled=True),
        lax.all_gather(w_down, ("seq", "ctx"), axis=0, tiled=True),
        lax.all_gather(mlp_gain, ("seq", "ctx"), axis=0, tiled=True),
    )
    normed_two, pull_two = jax.vjp(root_norm, resid, gain_mlp.astype(jnp.float32))
    low_two = normed_two.astype(jnp.bfloat16)
    gate = product(low_two, full_gate)
    upval = product(low_two, full_up)
    hidden, pull_hidden = jax.vjp(swiglu, gate, upval)
    hidden_low = hidden.astype(jnp.bfloat16)
    block_out = (resid + product(hidden_low, full_down)).astype(jnp.bfloat16)
    back_gate, back_up, back_down = (
        lax.all_gather(w_gate, ("seq", "ctx"), axis=0, tiled=True),
        lax.all_gather(w_up, ("seq", "ctx"), axis=0, tiled=True),
        lax.all_gather(w_down, ("seq", "ctx"), axis=0, tiled=True),
    )
    grad_hidden = product_right(upstream, back_down)
    grad_down = lax.psum_scatter(
        product_left(hidden_low, upstream), ("seq", "ctx"), scatter_dimension=0, tiled=True
    )
    grad_gate_act, grad_up_act = pull_hidden(grad_hidden)
    gate_low = grad_gate_act.astype(jnp.bfloat16)
    up_low = grad_up_act.astype(jnp.bfloat16)
    grad_normed_two = product_right(gate_low, back_gate) + product_right(up_low, back_up)
    resid_part, grad_gain_mlp = pull_two(grad_normed_two)
    grad_resid = upstream.astype(jnp.float32) + resid_part
    grad_gate, grad_up, grad_mlp_gain = (
        lax.psum_scatter(
            product_left(low_two, gate_low), ("seq", "ctx"), scatter_dimension=0, tiled=True
        ),
        lax.psum_scatter(
            product_left(low_two, up_low), ("seq", "ctx"), scatter_dimension=0, tiled=True
        ),
        lax.psum_scatter(grad_gain_mlp, ("seq", "ctx"), scatter_dimension=0, tiled=True),
    )
    back_query, back_key, back_value, back_out = (
        lax.all_gather(w_query, ("seq", "ctx"), axis=0, tiled=True),
        lax.all_gather(w_key, ("seq", "ctx"), axis=0, tiled=True),
        lax.all_gather(w_value, ("seq", "ctx"), axis=0, tiled=True),
        lax.all_gather(w_out, ("seq", "ctx"), axis=0, tiled=True),
    )
    resid_low = grad_resid.astype(jnp.bfloat16)
    grad_out_part = product_left(heads_low, resid_low)
    grad_heads = (
        product_right(resid_low, back_out)
        .astype(jnp.bfloat16)
        .reshape(rows, KV_HEADS, group, HEAD_DIM)
    )
    share_again = jnp.exp(score_block() - log_total)
    grad_share = jnp.einsum(
        "tkgd,skd->kgts", grad_heads, values_three, preferred_element_type=jnp.float32
    )
    grad_values_all = jnp.einsum(
        "kgts,tkgd->skd",
        share_again.astype(jnp.bfloat16),
        grad_heads,
        preferred_element_type=jnp.float32,
    )
    balance = jnp.sum(share_again * grad_share, axis=-1, keepdims=True)
    grad_scores = (share_again * (grad_share - balance)).astype(jnp.bfloat16)
    grad_query_rot = (
        jnp.einsum("kgts,skd->tkgd", grad_scores, keys_three, preferred_element_type=jnp.float32)
        * scale
    )
    grad_keys_all = (
        jnp.einsum("kgts,tkgd->skd", grad_scores, query_low, preferred_element_type=jnp.float32)
        * scale
    )
    grad_keys, grad_values = (
        lax.psum_scatter(
            grad_keys_all.reshape(length, KV_HEADS * HEAD_DIM),
            "ctx",
            scatter_dimension=0,
            tiled=True,
        ),
        lax.psum_scatter(
            grad_values_all.reshape(length, KV_HEADS * HEAD_DIM),
            "ctx",
            scatter_dimension=0,
            tiled=True,
        ),
    )
    grad_query_raw, grad_gain_query = pull_query(grad_query_rot.reshape(rows, HEADS, HEAD_DIM))
    grad_key_raw, grad_gain_key = pull_key(grad_keys.reshape(rows, KV_HEADS, HEAD_DIM))
    query_back = grad_query_raw.reshape(rows, HEADS * HEAD_DIM).astype(jnp.bfloat16)
    key_back = grad_key_raw.reshape(rows, KV_HEADS * HEAD_DIM).astype(jnp.bfloat16)
    value_back = grad_values.astype(jnp.bfloat16)
    grad_normed_one = (
        product_right(query_back, back_query)
        + product_right(key_back, back_key)
        + product_right(value_back, back_value)
    )
    input_part, grad_gain_attn = pull_one(grad_normed_one)
    grad_tokens = grad_resid + input_part
    grad_query, grad_key, grad_value, grad_out, grad_attn_gain, grad_query_gain, grad_key_gain = (
        lax.psum_scatter(
            product_left(low_one, query_back), ("seq", "ctx"), scatter_dimension=0, tiled=True
        ),
        lax.psum_scatter(
            product_left(low_one, key_back), ("seq", "ctx"), scatter_dimension=0, tiled=True
        ),
        lax.psum_scatter(
            product_left(low_one, value_back), ("seq", "ctx"), scatter_dimension=0, tiled=True
        ),
        lax.psum_scatter(grad_out_part, ("seq", "ctx"), scatter_dimension=0, tiled=True),
        lax.psum_scatter(grad_gain_attn, ("seq", "ctx"), scatter_dimension=0, tiled=True),
        lax.psum_scatter(grad_gain_query, ("seq", "ctx"), scatter_dimension=0, tiled=True),
        lax.psum_scatter(grad_gain_key, ("seq", "ctx"), scatter_dimension=0, tiled=True),
    )
    return (
        block_out[None],
        grad_tokens[None],
        grad_query,
        grad_key,
        grad_value,
        grad_out,
        grad_gate,
        grad_up,
        grad_down,
        grad_attn_gain,
        grad_mlp_gain,
        grad_query_gain,
        grad_key_gain,
    )


def solution(mesh):
    return jax.shard_map(
        body,
        mesh=mesh,
        in_specs=(
            P("seq", "ctx", None),
            P("seq", "ctx"),
            P("seq", "ctx", None),
            P(("seq", "ctx"), None),
            P(("seq", "ctx"), None),
            P(("seq", "ctx"), None),
            P(("seq", "ctx"), None),
            P(("seq", "ctx"), None),
            P(("seq", "ctx"), None),
            P(("seq", "ctx"), None),
            P(("seq", "ctx")),
            P(("seq", "ctx")),
            P(("seq", "ctx")),
            P(("seq", "ctx")),
        ),
        out_specs=(
            P("seq", "ctx", None),
            P("seq", "ctx", None),
            P(("seq", "ctx"), None),
            P(("seq", "ctx"), None),
            P(("seq", "ctx"), None),
            P(("seq", "ctx"), None),
            P(("seq", "ctx"), None),
            P(("seq", "ctx"), None),
            P(("seq", "ctx"), None),
            P(("seq", "ctx")),
            P(("seq", "ctx")),
            P(("seq", "ctx")),
            P(("seq", "ctx")),
        ),
        check_vma=False,
    )
```

profile of v0, /device:TPU:0, one launch (start us, length us, event | category | flops | bytes accessed | tf_op | source)
XLA Modules:
  0.0 3524.7 jit_solution(2357166484796503699)
XLA Ops:
  8.7 0.9 dynamic-update-slice.1
  9.6 0.8 dynamic-update-slice.2
  10.4 0.8 dynamic-update-slice
  12.1 42.2 %all-reduce.13 = (bf16[2048]{0:T(1024)(128)(2,1)S(1)}, bf16[128]{0:T(256)(128)(2,1)S(1)}, bf16[128]{0:T(256)(128)(2,1)S(1)}, bf16[2048]{0:T(1024)(128)(2,1)S(1)}) all-reduce(bf16[2048]{0:T(1024)(128)(2,1)S(1)} %dynamic-update-slice, bf16[128]{0:T(256)(128)(2,1)S(1)} %dynamic-update-slice.1, ...), channel_id=1, replica_groups=mesh['seq'=4,'ctx'=8] {'seq','ctx'}, use_global_device_ids=true, to_apply=%add.4 | all-reduce | flops 4352 | bytes 17408
  54.3 1.2 fusion.29
  55.6 20.3 all-gather.10.cloned.1.call-done
  75.8 3.8 convolution_convert_fusion.1
  80.5 59.1 %all-gather.14.cloned.1.call-done = bf16[2048,1024]{1,0:T(8,128)(2,1)} async-done(((bf16[64,1024]{1,0:T(8,128)(2,1)}), bf16[2048,1024]{1,0:T(8,128)(2,1)}) %all-gather.14.cloned.1.call-update) | async-done | bytes 4194320 | tf_op jit(solution)/shard_map/all_gather | solution.py:84
  139.6 6.6 copy.55
  146.2 3.6 multiply_reduce_fusion.8
  154.7 35.5 %all-gather.12.cloned.1.call-done = bf16[1024,1024]{1,0:T(8,128)(2,1)} async-done(((bf16[128,1024]{1,0:T(8,128)(2,1)}), bf16[1024,1024]{1,0:T(8,128)(2,1)}) %all-gather.12.cloned.1.call-update) | async-done | bytes 2097168 | tf_op jit(solution)/shard_map/all_gather | solution.py:103
  190.2 3.6 copy.87
  193.8 75.2 %all-gather.18.cloned.1.call-done = bf16[2048,2048]{1,0:T(8,128)(2,1)} async-done(((bf16[64,2048]{1,0:T(8,128)(2,1)}), bf16[2048,2048]{1,0:T(8,128)(2,1)}) %all-gather.18.cloned.1.call-update) | async-done | bytes 8388624 | tf_op jit(solution)/shard_map/all_gather | solution.py:83
  269.0 12.4 copy.56
  281.4 5.8 multiply_reduce_fusion.5
  288.2 33.0 all-gather.16.cloned.1.call-done
  321.1 3.5 fusion.69
  324.7 1.1 fusion.3
  325.8 2.4 copy-done
  328.2 2.2 fusion.22
  330.4 69.3 %all-gather.20.cloned.1.call-done = bf16[2048,2048]{1,0:T(8,128)(2,1)} async-done(((bf16[64,2048]{1,0:T(8,128)(2,1)}), bf16[2048,2048]{1,0:T(8,128)(2,1)}) %all-gather.20.cloned.1.call-update) | async-done | bytes 8388624 | tf_op jit(solution)/shard_map/all_gather | solution.py:86
  399.7 4.7 multiply_reduce_fusion.4
  404.6 151.3 %all-gather.24.cloned.1.call-done = bf16[2048,6144]{1,0:T(8,128)(2,1)} async-done(((bf16[64,6144]{1,0:T(8,128)(2,1)}), bf16[2048,6144]{1,0:T(8,128)(2,1)}) %all-gather.24.cloned.1.call-update) | async-done | bytes 25165840 | tf_op jit(solution)/shard_map/all_gather | solution.py:134
  555.9 13.3 fusion.71
  569.3 142.5 %all-gather.22.cloned.1.call-done = bf16[2048,6144]{1,0:T(8,128)(2,1)} async-done(((bf16[64,6144]{1,0:T(8,128)(2,1)}), bf16[2048,6144]{1,0:T(8,128)(2,1)}) %all-gather.22.cloned.1.call-update) | async-done | bytes 25165840 | tf_op jit(solution)/shard_map/all_gather | solution.py:133
  711.8 13.2 fusion.70
  725.0 142.6 %all-gather.26.cloned.1.call-done = bf16[6144,2048]{1,0:T(8,128)(2,1)} async-done(((bf16[192,2048]{1,0:T(8,128)(2,1)}), bf16[6144,2048]{1,0:T(8,128)(2,1)}) %all-gather.26.cloned.1.call-update) | async-done | bytes 25165840 | tf_op jit(solution)/shard_map/all_gather | solution.py:135
  867.6 16.9 multiply_convert_fusion
  884.6 14.7 fusion.72
  899.3 15.3 multiply_reduce_fusion.1
  914.5 1.7 fusion.33
  916.2 1.0 copy-done.7
  917.2 6.3 convolution_convert_fusion
  923.8 6.9 fusion.5
  930.7 5.9 fusion
  936.6 4.6 fusion.2
  941.2 3.7 bitcast_multiply_fusion.1
  945.0 72.4 %reduce-scatter.12.cloned.1.call-done = f32[128,1024]{0,1:T(8,128)} async-done(((f32[1024,1024]{0,1:T(8,128)}), f32[128,1024]{0,1:T(8,128)}) %reduce-scatter.12.cloned.1.call-update) | async-done | bytes 524304 | tf_op jit(solution)/shard_map/reduce_scatter | solution.py:209
  1017.4 5.6 fusion.54
  1023.1 86.7 %reduce-scatter.10.cloned.1.call-done = f32[128,1024]{0,1:T(8,128)} async-done(((f32[1024,1024]{0,1:T(8,128)}), f32[128,1024]{0,1:T(8,128)}) %reduce-scatter.10.cloned.1.call-update) | async-done | bytes 524304 | tf_op jit(solution)/shard_map/reduce_scatter | solution.py:203
  1109.8 1.1 multiply_add_fusion.3
  1111.2 4.7 fusion.46
  1116.0 1.1 copy-done.8
  1117.1 9.1 fusion.51
  1126.3 3.6 convolution_multiply_fusion
  1131.8 8.2 fusion.48
  1140.0 1.0 copy-done.20
  1141.0 21.3 fusion.38
  1162.3 21.1 fusion.75
  1183.5 21.1 fusion.74
  1204.6 1.0 copy-done.18
  1205.6 6.5 fusion.73
  1212.1 11.2 fusion.14
  1223.4 1.5 convolution_add_fusion.1
  1225.7 1.7 fusion.28
  1227.4 46.1 %all-reduce.12 = (f32[2048]{0:T(1024)S(1)}, f32[2048]{0:T(1024)S(1)}, f32[128]{0:T(128)S(1)}, f32[128]{0:T(128)S(1)}) all-reduce(f32[2048]{0:T(1024)S(1)} %get-tuple-element.17, f32[2048]{0:T(1024)S(1)} %copy-done.22, f32[128]{0:T(128)S(1)} %get-tuple-element.13, ...), channel_id=11, replica_groups=mesh['seq'=4,'ctx'=8] {'seq','ctx'}, use_global_device_ids=true, to_apply=%region_21.22.clone | all-reduce | flops 4352 | bytes 34816
  1275.9 1.3 fusion.36
  1277.2 21.1 reduce-scatter.18.cloned.1.call-done
  1298.3 186.9 %reduce-scatter.16.cloned.1.call-done = f32[64,1024]{1,0:T(8,128)} async-done(((f32[2048,1024]{1,0:T(8,128)}), f32[64,1024]{1,0:T(8,128)}) %reduce-scatter.16.cloned.1.call-update) | async-done | bytes 262160 | tf_op jit(solution)/shard_map/reduce_scatter | solution.py:232
  1485.2 359.9 %reduce-scatter.20.cloned.1.call-done = f32[64,2048]{1,0:T(8,128)} async-done(((f32[2048,2048]{1,0:T(8,128)}), f32[64,2048]{1,0:T(8,128)}) %reduce-scatter.20.cloned.1.call-update) | async-done | bytes 524304 | tf_op jit(solution)/shard_map/reduce_scatter | solution.py:238
  1845.1 360.1 %reduce-scatter.14.cloned.1.call-done = f32[64,2048]{1,0:T(8,128)} async-done(((f32[2048,2048]{1,0:T(8,128)}), f32[64,2048]{1,0:T(8,128)}) %reduce-scatter.14.cloned.1.call-update) | async-done | bytes 524304 | tf_op jit(solution)/shard_map/reduce_scatter | solution.py:229
  2205.2 437.7 %reduce-scatter.26.cloned.1.call-done = f32[192,2048]{1,0:T(8,128)} async-done(((f32[6144,2048]{1,0:T(8,128)}), f32[192,2048]{1,0:T(8,128)}) %reduce-scatter.26.cloned.1.call-update) | async-done | bytes 1572880 | tf_op jit(solution)/shard_map/reduce_scatter | solution.py:151
  2642.9 437.3 %reduce-scatter.24.cloned.1.call-done = f32[64,6144]{1,0:T(8,128)} async-done(((f32[2048,6144]{1,0:T(8,128)}), f32[64,6144]{1,0:T(8,128)}) %reduce-scatter.24.cloned.1.call-update) | async-done | bytes 1572880 | tf_op jit(solution)/shard_map/reduce_scatter | solution.py:164
  3080.1 437.5 %reduce-scatter.22.cloned.1.call-done = f32[64,6144]{1,0:T(8,128)} async-done(((f32[2048,6144]{1,0:T(8,128)}), f32[64,6144]{1,0:T(8,128)}) %reduce-scatter.22.cloned.1.call-update) | async-done | bytes 1572880 | tf_op jit(solution)/shard_map/reduce_scatter | solution.py:161
  (124 shorter events, 15.2 us)
Async XLA Ops:
  7.2 73.1 %copy-start.25 = (s32[1,128]{1,0:T(1,128)S(1)}, s32[1,128]{1,0:T(1,128)}, u32[]{:S(2)}) copy-start(s32[1,128]{1,0:T(1,128)} %param.15) | copy-start | bytes 1540
  7.2 68.6 %all-gather.10.cloned.1.call-start = ((), (), s32[]{:S(2)}) async-start(), calls=%async_computation.9 | async-start | bytes 4325376 | tf_op jit(solution)/shard_map/all_gather | solution.py:85
  7.9 131.7 %all-gather.14.cloned.1.call-start = ((), (), s32[]{:S(2)}) async-start(), calls=%async_computation.11 | async-start | bytes 4325376 | tf_op jit(solution)/shard_map/all_gather | solution.py:84
  8.7 181.5 %all-gather.12.cloned.1.call-start = ((), (), s32[]{:S(2)}) async-start(), calls=%async_computation.10 | async-start | bytes 2359296 | tf_op jit(solution)/shard_map/all_gather | solution.py:103
  55.5 24.8 copy-start.23
  79.7 189.3 %all-gather.18.cloned.1.call-start = ((), (), s32[]{:S(2)}) async-start(), calls=%async_computation.13 | async-start | bytes 8650752 | tf_op jit(solution)/shard_map/all_gather | solution.py:83
  80.2 240.9 %all-gather.16.cloned.1.call-start = ((), (), s32[]{:S(2)}) async-start(), calls=%async_computation.12 | async-start | bytes 2359296 | tf_op jit(solution)/shard_map/all_gather | solution.py:102
  139.6 6.6 copy-start.1
  149.8 0.8 copy-start.11
  151.5 248.2 %all-gather.20.cloned.1.call-start = ((), (), s32[]{:S(2)}) async-start(), calls=%async_computation.14 | async-start | bytes 8650752 | tf_op jit(solution)/shard_map/all_gather | solution.py:86
  152.1 403.8 %all-gather.24.cloned.1.call-start = ((), (), s32[]{:S(2)}) async-start(), calls=%async_computation.16 | async-start | bytes 25952256 | tf_op jit(solution)/shard_map/all_gather | solution.py:134
  152.9 558.9 %all-gather.22.cloned.1.call-start = ((), (), s32[]{:S(2)}) async-start(), calls=%async_computation.15 | async-start | bytes 25952256 | tf_op jit(solution)/shard_map/all_gather | solution.py:133
  153.6 714.0 %all-gather.26.cloned.1.call-start = ((), (), s32[]{:S(2)}) async-start(), calls=%async_computation.17 | async-start | bytes 25952256 | tf_op jit(solution)/shard_map/all_gather | solution.py:135
  154.3 863.1 %reduce-scatter.12.cloned.1.call-start = ((), (), s32[]{:S(2)}) async-start(), calls=%async_computation.19 | async-start | bytes 4718592 | tf_op jit(solution)/shard_map/reduce_scatter | solution.py:209
  287.9 36.7 %copy-start.13 = (bf16[128,8,2,64]{3,0,2,1:T(8,128)(2,1)}, bf16[128,8,2,64]{3,0,2,1:T(8,128)(2,1)S(1)}, u32[]{:S(2)}) copy-start(bf16[128,8,2,64]{3,0,2,1:T(8,128)(2,1)S(1)} %copy.58) | copy-start | bytes 786436
  288.2 36.5 %copy-start.15 = (bf16[128,8,2,64]{3,0,2,1:T(8,128)(2,1)}, bf16[128,8,2,64]{3,0,2,1:T(8,128)(2,1)S(1)}, u32[]{:S(2)}) copy-start(bf16[128,8,2,64]{3,0,2,1:T(8,128)(2,1)S(1)} %copy.57) | copy-start | bytes 786436
  324.6 3.5 copy-start
  324.7 3.5 copy-start.9
  330.4 74.1 %copy-start.19 = (bf16[8,128,2,128]{3,1,2,0:T(8,128)(2,1)}, bf16[8,128,2,128]{3,1,2,0:T(8,128)(2,1)S(1)}, u32[]{:S(2)}) copy-start(bf16[8,128,2,128]{3,1,2,0:T(8,128)(2,1)S(1)} %fusion.22) | copy-start | bytes 1572868
  404.4 510.1 %copy-start.3 = (f32[128,2048]{1,0:T(8,128)}, f32[128,2048]{1,0:T(8,128)S(1)}, u32[]{:S(2)}) copy-start(f32[128,2048]{1,0:T(8,128)S(1)} %get-tuple-element.49) | copy-start | bytes 3145732
  916.2 1.0 copy-start.7
  930.6 179.1 %reduce-scatter.10.cloned.1.call-start = ((), (), s32[]{:S(2)}) async-start(), calls=%async_computation.18 | async-start | bytes 4718592 | tf_op jit(solution)/shard_map/reduce_scatter | solution.py:203
  936.6 4.6 copy-start.14
  936.6 4.6 copy-start.16
  941.2 3.7 copy-start.2
  945.0 353.3 %reduce-scatter.18.cloned.1.call-start = ((), (), s32[]{:S(2)}) async-start(), calls=%async_computation.22 | async-start | bytes 8650752 | tf_op jit(solution)/shard_map/reduce_scatter | solution.py:235
  1023.1 87.8 %copy-start.12 = (f32[128,8,128]{0,2,1:T(8,128)S(1)}, f32[128,8,128]{0,2,1:T(8,128)}, u32[]{:S(2)}) copy-start(f32[128,8,128]{0,2,1:T(8,128)} %copy-done.11) | copy-start | bytes 1572868
  1023.1 462.1 %reduce-scatter.16.cloned.1.call-start = ((), (), s32[]{:S(2)}) async-start(), calls=%async_computation.21 | async-start | bytes 8650752 | tf_op jit(solution)/shard_map/reduce_scatter | solution.py:232
  1115.9 1.2 copy-start.8
  1115.9 729.2 %reduce-scatter.20.cloned.1.call-start = ((), (), s32[]{:S(2)}) async-start(), calls=%async_computation.23 | async-start | bytes 17301504 | tf_op jit(solution)/shard_map/reduce_scatter | solution.py:238
  1126.3 1078.9 %reduce-scatter.14.cloned.1.call-start = ((), (), s32[]{:S(2)}) async-start(), calls=%async_computation.20 | async-start | bytes 17301504 | tf_op jit(solution)/shard_map/reduce_scatter | solution.py:229
  1131.0 0.8 copy-start.17
  1139.9 1.0 copy-start.20
  1140.0 1502.9 %reduce-scatter.26.cloned.1.call-start = ((), (), s32[]{:S(2)}) async-start(), calls=%async_computation.26 | async-start | bytes 51904512 | tf_op jit(solution)/shard_map/reduce_scatter | solution.py:151
  1162.3 1917.9 %reduce-scatter.24.cloned.1.call-start = ((), (), s32[]{:S(2)}) async-start(), calls=%async_computation.25 | async-start | bytes 51904512 | tf_op jit(solution)/shard_map/reduce_scatter | solution.py:164
  1183.4 2334.2 %reduce-scatter.22.cloned.1.call-start = ((), (), s32[]{:S(2)}) async-start(), calls=%async_computation.24 | async-start | bytes 51904512 | tf_op jit(solution)/shard_map/reduce_scatter | solution.py:161
  1204.6 1.0 copy-start.18
  1205.6 6.5 copy-start.4
  1205.6 6.5 copy-start.10
  1212.1 11.2 copy-start.6
  1223.4 2.2 copy-start.5
  1223.4 2.3 copy-start.21
  1225.7 1.7 copy-start.22
  1225.7 50.2 %copy-start.24 = (f32[128]{0:T(128)S(1)}, f32[128]{0:T(128)}, u32[]{:S(2)}) copy-start(f32[128]{0:T(128)} %copy-done.23) | copy-start | bytes 1540
Sparse Core Ops, SparseCore 0:
  11.0 64.7 all-gather.9
  78.8 60.7 all-gather.13
  142.3 47.8 all-gather.11
  193.0 75.8 all-gather.17
  271.4 49.6 all-gather.15
  324.0 75.6 all-gather.19
  402.7 153.2 all-gather.23
  558.9 152.8 all-gather.21
  714.8 152.8 all-gather.25
  930.8 86.6 reduce-scatter.11
  1021.5 88.2 reduce-scatter.9
  1112.5 185.7 reduce-scatter.17
  1301.2 183.9 reduce-scatter.15
  1487.9 357.1 reduce-scatter.19
  1847.8 357.3 reduce-scatter.13
  2212.0 430.7 reduce-scatter.25
  2649.7 430.3 reduce-scatter.23
  3087.0 430.5 reduce-scatter.21
where the time goes:
time: 3530 us; the launch traced here: 3520 us
  waiting for transfers between devices  3130 us (89%)
  matrix products  235 us (7%)
  blocking collectives  88.3 us (3%)
  local copies, waits for them, and re-layouts  38 us (1%)
    reduce_scatter x1, waiting for transfers between devices, body(): lax.psum_scatter(product_left(hidden_low, upstream), ('seq', 'ctx'), scat...  438 us
    reduce_scatter x1, waiting for transfers between devices, body(): lax.psum_scatter(product_left(low_two, gate_low), ('seq', 'ctx'), scatter...  437 us
    reduce_scatter x1, waiting for transfers between devices, body(): lax.psum_scatter(product_left(low_two, up_low), ('seq', 'ctx'), scatter_d...  437 us
    reduce_scatter x1, waiting for transfers between devices, body(): lax.psum_scatter(product_left(low_one, query_back), ('seq', 'ctx'), scatt...  360 us
    reduce_scatter x1, waiting for transfers between devices, body(): lax.psum_scatter(grad_out_part, ('seq', 'ctx'), scatter_dimension=0, tile...  360 us
    reduce_scatter x1, waiting for transfers between devices, body(): lax.psum_scatter(product_left(low_one, key_back), ('seq', 'ctx'), scatter...  187 us
    all_gather x1, waiting for transfers between devices, body(): lax.all_gather(w_up, ('seq', 'ctx'), axis=0, tiled=True)  151 us
    all_gather x1, waiting for transfers between devices, body(): lax.all_gather(w_down, ('seq', 'ctx'), axis=0, tiled=True)  143 us
  transfers between devices with their start and end apart: 18, of which 18 were waited for; matrix products, arithmetic and copies ran while one was open for 6% of the time, Pallas kernels for 0%

commit v1 on v0

--- a/solution.py
+++ b/solution.py
@@ -3,6 +3,8 @@
 import jax
 import jax.numpy as jnp
 from jax import lax
+from jax.experimental import pallas as pl
+from jax.experimental.pallas import tpu as pltpu
 from jax.sharding import PartitionSpec as P
 
 HEADS = 16
@@ -56,7 +58,7 @@
     )
 
 
-def body(
+def whole_body(
     tokens,
     positions,
     cotangent,
@@ -257,9 +259,848 @@
     )
 
 
+def head_order(parts):
+    half = parts // 2
+    return [2 * (c % half) + c // half for c in range(parts)]
+
+
+PAD = 16
+DIGIT = 128
+
+
+def fold_qkv_kernel(parts, query, key, value, gains, positions, out):
+    own = query.shape[0]
+    group = query.shape[1] // parts
+    head = key.shape[1] // parts
+    where = positions[...]
+    high = (where >> 7).astype(jnp.float32).astype(jnp.bfloat16)
+    rest = (where & (DIGIT - 1)).astype(jnp.float32).astype(jnp.bfloat16)
+    rows = where.shape[1]
+    count = gains.shape[1]
+    for c, k in enumerate(head_order(parts)):
+        out[c, :own, :group] = query[:, k * group : (k + 1) * group]
+        out[c, :own, group : group + head] = key[:, k * head : (k + 1) * head]
+        out[c, :own, group + head :] = value[:, k * head : (k + 1) * head]
+        out[c, own:, :] = jnp.zeros((PAD, out.shape[2]), out.dtype)
+        out[c, own : own + 1, :count] = gains[...]
+        out[c, own + 1 : own + 2, :rows] = high
+        out[c, own + 1 : own + 2, rows : 2 * rows] = rest
+
+
+def fold_qkv(w_query, w_key, w_value, gains, positions, parts):
+    own = w_query.shape[0]
+    cols = (w_query.shape[1] + w_key.shape[1] + w_value.shape[1]) // parts
+    return pl.pallas_call(
+        partial(fold_qkv_kernel, parts),
+        out_shape=jax.ShapeDtypeStruct((parts, own + PAD, cols), w_query.dtype),
+        cost_estimate=pl.CostEstimate(flops=0, bytes_accessed=1200000, transcendentals=0),
+    )(w_query, w_key, w_value, gains, positions)
+
+
+def fold_ff_kernel(seqs, parts, gate, up, out):
+    unit = gate.shape[1] // (seqs * parts)
+    for c in range(parts):
+        for s in range(seqs):
+            at = (s * parts + c) * unit
+            out[c, :, s * unit : (s + 1) * unit] = gate[:, at : at + unit]
+            out[c, :, (seqs + s) * unit : (seqs + s + 1) * unit] = up[:, at : at + unit]
+
+
+def fold_ff(w_gate, w_up, seqs, parts):
+    own, hidden = w_gate.shape
+    return pl.pallas_call(
+        partial(fold_ff_kernel, seqs, parts),
+        out_shape=jax.ShapeDtypeStruct((parts, own, 2 * hidden // parts), w_gate.dtype),
+        cost_estimate=pl.CostEstimate(flops=0, bytes_accessed=3200000, transcendentals=0),
+    )(w_gate, w_up)
+
+
+def unfold_ff_kernel(seqs, parts, turned, gate, up):
+    unit = gate.shape[1] // (seqs * parts)
+    for c in range(parts):
+        for s in range(seqs):
+            at = (s * parts + c) * unit
+            gate[:, at : at + unit] = turned[c, :, s * unit : (s + 1) * unit].astype(gate.dtype)
+            up[:, at : at + unit] = turned[
+                c, :, (seqs + s) * unit : (seqs + s + 1) * unit
+            ].astype(up.dtype)
+
+
+def unfold_ff(turned, seqs, parts):
+    own = turned.shape[1]
+    shape = jax.ShapeDtypeStruct((own, turned.shape[2] * parts // 2), jnp.float32)
+    return pl.pallas_call(
+        partial(unfold_ff_kernel, seqs, parts),
+        out_shape=(shape, shape),
+        cost_estimate=pl.CostEstimate(flops=0, bytes_accessed=5000000, transcendentals=0),
+    )(turned)
+
+
+def unfold_qkv_kernel(turned, query, key, value, gains):
+    parts = turned.shape[0]
+    own = query.shape[0]
+    group = query.shape[1] // parts
+    head = key.shape[1] // parts
+    total = jnp.zeros((1, turned.shape[2]), jnp.float32)
+    for c, k in enumerate(head_order(parts)):
+        query[:, k * group : (k + 1) * group] = turned[c, :own, :group].astype(jnp.float32)
+        key[:, k * head : (k + 1) * head] = turned[c, :own, group : group + head].astype(
+            jnp.float32
+        )
+        value[:, k * head : (k + 1) * head] = turned[c, :own, group + head :].astype(jnp.float32)
+        total = total + turned[c, own:, :].astype(jnp.float32)[:1]
+    gains[...] = total
+
+
+def unfold_qkv(turned, own):
+    parts, _, cols = turned.shape
+    group = cols * HEADS // (HEADS + 2 * KV_HEADS)
+    head = (cols - group) // 2
+    return pl.pallas_call(
+        unfold_qkv_kernel,
+        out_shape=(
+            jax.ShapeDtypeStruct((own, parts * group), jnp.float32),
+            jax.ShapeDtypeStruct((own, parts * head), jnp.float32),
+            jax.ShapeDtypeStruct((own, parts * head), jnp.float32),
+            jax.ShapeDtypeStruct((1, cols), jnp.float32),
+        ),
+        cost_estimate=pl.CostEstimate(flops=0, bytes_accessed=1900000, transcendentals=0),
+    )(turned)
+
+
+ROWS = 256
+
+
+def turn_halves(value):
+    return pltpu.roll(value, value.shape[1] // 2, 1)
+
+
+def dot_right(left, right):
+    return lax.dot_general(
+        left, right, (((1,), (1,)), ((), ())), preferred_element_type=jnp.float32
+    )
+
+
+def dot_left(left, right):
+    return lax.dot_general(
+        left, right, (((0,), (0,)), ((), ())), preferred_element_type=jnp.float32
+    )
+
+
+def project_kernel(
+    own, tokens, gathered, gain, cosine, sine, gain_query, gain_key,
+    normed, raw, query, key, value, weight,
+):
+    head = gain_query.shape[1]
+    group = query.shape[1] // head
+
+    @pl.when(pl.program_id(0) == 0)
+    def _():
+        weight[...] = gathered[:, :own, :].reshape(weight.shape)
+
+    x = tokens[...].astype(jnp.float32)
+    low = root_norm(x, gain[...]).astype(jnp.bfloat16)
+    normed[...] = low
+    qkv = jnp.dot(low, weight[...], preferred_element_type=jnp.float32)
+    raw[...] = qkv[:, : (group + 1) * head]
+    value[...] = qkv[:, (group + 1) * head :].astype(jnp.bfloat16)
+    cos = cosine[...]
+    sin = sine[...]
+    for h in range(group + 1):
+        scale = gain_key[...] if h == group else gain_query[...]
+        part = root_norm(qkv[:, h * head : (h + 1) * head], scale)
+        part = (part * cos + turn_halves(part) * sin).astype(jnp.bfloat16)
+        if h == group:
+            key[...] = part
+        else:
+            query[:, h * head : (h + 1) * head] = part
+
+
+def project(tokens, gathered, gain, cosine, sine, gain_query, gain_key, own):
+    length, width = tokens.shape
+    cols = gathered.shape[2]
+    head = gain_query.shape[1]
+    rows = min(ROWS, length)
+
+    def block(n):
+        return pl.BlockSpec((rows, n), lambda i: (i, 0))
+
+    def whole(*shape):
+        return pl.BlockSpec(shape, lambda i: (0,) * len(shape))
+
+    def out(n, kind=jnp.bfloat16):
+        return jax.ShapeDtypeStruct((length, n), kind)
+
+    raw_cols = cols - head
+    return pl.pallas_call(
+        partial(project_kernel, own),
+        grid=(length // rows,),
+        in_specs=[
+            block(width),
+            whole(*gathered.shape),
+            whole(1, width),
+            block(head),
+            block(head),
+            whole(1, head),
+            whole(1, head),
+        ],
+        out_specs=[
+            block(width),
+            block(raw_cols),
+            block(raw_cols - head),
+            block(head),
+            block(head),
+            whole(width, cols),
+        ],
+        out_shape=[
+            out(width),
+            out(raw_cols, jnp.float32),
+            out(raw_cols - head),
+            out(head),
+            out(head),
+            jax.ShapeDtypeStruct((width, cols), jnp.bfloat16),
+        ],
+        cost_estimate=pl.CostEstimate(
+            flops=2 * length * width * cols, bytes_accessed=14000000, transcendentals=0
+        ),
+        compiler_params=pltpu.CompilerParams(vmem_limit_bytes=24 * 2**20),
+    )(tokens, gathered, gain, cosine, sine, gain_query, gain_key)
+
+
+def block_mask(start, first, rows, keys):
+    spot = first + lax.broadcasted_iota(jnp.int32, (rows, keys), 0)
+    other = lax.broadcasted_iota(jnp.int32, (rows, keys), 1)
+    return (other <= spot) & (other >= start)
+
+
+def attend_kernel(query, key, value, start, heads, lse):
+    length = query.shape[0]
+    head = key.shape[1]
+    rows = min(ROWS, length)
+    scale = head ** (-0.5)
+    for i in range(length // rows):
+        at = slice(i * rows, (i + 1) * rows)
+        keys = (i + 1) * rows
+        visible = block_mask(start[at, :], i * rows, rows, keys)
+        for h in range(query.shape[1] // head):
+            of = slice(h * head, (h + 1) * head)
+            scores = dot_right(query[at, of], key[:keys, :]) * scale
+            scores = jnp.where(visible, scores, NEG)
+            peak = jnp.max(scores, axis=1, keepdims=True)
+            powers = jnp.exp(scores - peak)
+            total = jnp.sum(powers, axis=1, keepdims=True)
+            share = (powers / total).astype(jnp.bfloat16)
+            heads[at, of] = jnp.dot(
+                share, value[:keys, :], preferred_element_type=jnp.float32
+            ).astype(jnp.bfloat16)
+            lse[at, h : h + 1] = peak + jnp.log(total)
+
+
+def attend(query, key, value, start):
+    length, cols = query.shape
+    return pl.pallas_call(
+        attend_kernel,
+        out_shape=(
+            jax.ShapeDtypeStruct((length, cols), jnp.bfloat16),
+            jax.ShapeDtypeStruct((length, cols // key.shape[1]), jnp.float32),
+        ),
+        cost_estimate=pl.CostEstimate(
+            flops=4 * length * length * cols, bytes_accessed=2600000, transcendentals=2 * length * length
+        ),
+        compiler_params=pltpu.CompilerParams(vmem_limit_bytes=24 * 2**20),
+    )(query, key, value, start)
+
+
+def norm_back(raw, gain, grad):
+    r = lax.rsqrt(jnp.mean(raw * raw, axis=1, keepdims=True) + EPS)
+    weighted = gain * grad
+    back = r * weighted - (r * r * r) * raw * jnp.mean(weighted * raw, axis=1, keepdims=True)
+    return back, jnp.sum(grad * raw * r, axis=0, keepdims=True)
+
+
+def attend_back_kernel(
+    query, key, value, start, lse, grads, raw, cosine, sine, gain_query, gain_key,
+    back, part_query, part_key, grad_key, grad_value,
+):
+    length = query.shape[0]
+    head = key.shape[1]
+    group = query.shape[1] // head
+    rows = min(ROWS, length)
+    scale = head ** (-0.5)
+    low = jnp.bfloat16
+    grad_key[...] = jnp.zeros_like(grad_key)
+    grad_value[...] = jnp.zeros_like(grad_value)
+    total_query = jnp.zeros((1, head), jnp.float32)
+    total_key = jnp.zeros((1, head), jnp.float32)
+    for i in range(length // rows):
+        at = slice(i * rows, (i + 1) * rows)
+        keys = (i + 1) * rows
+        visible = block_mask(start[at, :], i * rows, rows, keys)
+        cos = cosine[at, :]
+        sin = sine[at, :]
+        for h in range(group):
+            of = slice(h * head, (h + 1) * head)
+            one = query[at, of]
+            grad = grads[at, of]
+            scores = jnp.where(visible, dot_right(one, key[:keys, :]) * scale, NEG)
+            share = jnp.exp(scores - lse[at, h : h + 1])
+            grad_share = dot_right(grad, value[:keys, :])
+            grad_value[:keys, :] += dot_left(share.astype(low), grad)
+            balance = jnp.sum(share * grad_share, axis=1, keepdims=True)
+            grad_scores = (share * (grad_share - balance)).astype(low)
+            turned = (
+                jnp.dot(grad_scores, key[:keys, :], preferred_element_type=jnp.float32) * scale
+            )
+            grad_key[:keys, :] += dot_left(grad_scores, one)
+            turned = turned * cos - turn_halves(turned) * sin
+            result, term = norm_back(raw[at, of], gain_query[...], turned)
+            back[at, of] = result.astype(low)
+            total_query += term
+    of = slice(group * head, (group + 1) * head)
+    for i in range(length // rows):
+        at = slice(i * rows, (i + 1) * rows)
+        turned = grad_key[at, :] * scale
+        turned = turned * cosine[at, :] - turn_halves(turned) * sine[at, :]
+        result, term = norm_back(raw[at, of], gain_key[...], turned)
+        back[at, of] = result.astype(low)
+        total_key += term
+        back[at, (group + 1) * head :] = grad_value[at, :].astype(low)
+    part_query[...] = total_query
+    part_key[...] = total_key
+
+
+def attend_back(query, key, value, start, lse, grads, raw, cosine, sine, gain_query, gain_key):
+    length, cols = query.shape
+    head = key.shape[1]
+    row = jax.ShapeDtypeStruct((1, head), jnp.float32)
+    return pl.pallas_call(
+        attend_back_kernel,
+        out_shape=(
+            jax.ShapeDtypeStruct((length, cols + 2 * head), jnp.bfloat16),
+            row,
+            row,
+        ),
+        scratch_shapes=[
+            pltpu.VMEM((length, head), jnp.float32),
+            pltpu.VMEM((length, head), jnp.float32),
+        ],
+        cost_estimate=pl.CostEstimate(
+            flops=10 * length * length * cols, bytes_accessed=6000000, transcendentals=2 * length * length
+        ),
+        compiler_params=pltpu.CompilerParams(vmem_limit_bytes=28 * 2**20),
+    )(query, key, value, start, lse, grads, raw, cosine, sine, gain_query, gain_key)
+
+
+def pack_grads_kernel(own, normed, back, attn, mlp, query, key, out):
+    owners = out.shape[0]
+    small = query.shape[1] // owners
+    low = out.dtype
+    cols = out.shape[2]
+    chunk = min(owners, 4)
+    for first in range(0, owners, chunk):
+        part = dot_left(normed[:, first * own : (first + chunk) * own], back[...]).astype(low)
+        out[first : first + chunk, :own, :] = part.reshape(chunk, own, cols)
+    out[:, own:, :] = jnp.zeros((owners, PAD, cols), low)
+    for o in range(owners):
+        row = slice(own, own + 1)
+        out[o, row, :own] = attn[:, o * own : (o + 1) * own].astype(low)
+        out[o, row, own : 2 * own] = mlp[:, o * own : (o + 1) * own].astype(low)
+        out[o, row, 2 * own : 2 * own + small] = query[:, o * small : (o + 1) * small].astype(low)
+        out[o, row, 2 * own + small : 2 * (own + small)] = key[
+            :, o * small : (o + 1) * small
+        ].astype(low)
+
+
+def pack_grads(normed, back, attn, mlp, query, key, own):
+    length, width = normed.shape
+    cols = back.shape[1]
+    owners = width // own
+    return pl.pallas_call(
+        partial(pack_grads_kernel, own),
+        out_shape=jax.ShapeDtypeStruct((owners, own + PAD, cols), jnp.bfloat16),
+        cost_estimate=pl.CostEstimate(
+            flops=2 * length * width * cols, bytes_accessed=8000000, transcendentals=0
+        ),
+        compiler_params=pltpu.CompilerParams(vmem_limit_bytes=24 * 2**20),
+    )(normed, back, attn, mlp, query, key).reshape(-1, cols)
+
+
+def feed_kernel(count, *refs):
+    arrived = refs[:count]
+    upstream = refs[count : 2 * count]
+    w_gu, w_down, hidden_out, gate_out, up_out, part_out, part_two = refs[2 * count :]
+    low = jnp.bfloat16
+    wide = w_down.shape[0]
+
+    def join(pieces):
+        return jnp.concatenate([piece[...] for piece in pieces], axis=0)
+
+    normed = join(arrived)
+    gate = jnp.dot(normed, w_gu[:, :wide], preferred_element_type=jnp.float32)
+    up = jnp.dot(normed, w_gu[:, wide:], preferred_element_type=jnp.float32)
+    grad_hidden = dot_right(join(upstream), w_down[...])
+    s = jax.nn.sigmoid(gate)
+    silu = gate * s
+    hidden = (silu * up).astype(low)
+    grad_gate = (grad_hidden * up * s * (1.0 + gate * (1.0 - s))).astype(low)
+    grad_up = (grad_hidden * silu).astype(low)
+    hidden_out[...] = hidden
+    gate_out[...] = grad_gate
+    up_out[...] = grad_up
+    part_out[...] = jnp.dot(hidden, w_down[...], preferred_element_type=jnp.float32).astype(low)
+    part_two[...] = (
+        dot_right(grad_gate, w_gu[:, :wide]) + dot_right(grad_up, w_gu[:, wide:])
+    ).astype(low)
+
+
+def feed(arrived, upstream, w_gu, w_down):
+    count = len(arrived)
+    wide, width = w_down.shape
+    rows = sum(item.shape[0] for item in arrived)
+    low = jnp.bfloat16
+    return pl.pallas_call(
+        partial(feed_kernel, count),
+        out_shape=[jax.ShapeDtypeStruct((rows, wide), low)] * 3
+        + [jax.ShapeDtypeStruct((rows, width), low)] * 2,
+        cost_estimate=pl.CostEstimate(
+            flops=12 * rows * width * wide,
+            bytes_accessed=6 * width * wide + 12 * rows * width,
+            transcendentals=rows * wide,
+        ),
+        compiler_params=pltpu.CompilerParams(vmem_limit_bytes=22 * 2**20),
+    )(*arrived, *upstream, w_gu, w_down)
+
+
+def outer_kernel(counts, rights, *refs):
+    out = refs[-1]
+    at = 0
+    lefts = []
+    for count in counts:
+        lefts.append(jnp.concatenate([item[...] for item in refs[at : at + count]], axis=0))
+        at += count
+    first = 0
+    for sizes in rights:
+        total = None
+        for left, size in zip(lefts, sizes):
+            right = jnp.concatenate([item[...] for item in refs[at : at + size]], axis=0)
+            at += size
+            term = dot_left(left, right)
+            total = term if total is None else total + term
+        out[:, first : first + total.shape[1]] = total.astype(out.dtype)
+        first += total.shape[1]
+
+
+def outer_sum(lefts, rights, tile):
+    flat_left = [item for group in lefts for item in group]
+    flat_right = [item for side in rights for group in side for item in group]
+    tall = flat_left[0].shape[1]
+    cols = sum(side[0][0].shape[1] for side in rights)
+    length = sum(item.shape[0] for item in flat_left)
+    return pl.pallas_call(
+        partial(
+            outer_kernel,
+            [len(group) for group in lefts],
+            [[len(group) for group in side] for side in rights],
+        ),
+        grid=(tall // tile,),
+        in_specs=[pl.BlockSpec((item.shape[0], tile), lambda i: (0, i)) for item in flat_left]
+        + [pl.BlockSpec(item.shape, lambda i: (0, 0)) for item in flat_right],
+        out_specs=pl.BlockSpec((tile, cols), lambda i: (i, 0)),
+        out_shape=jax.ShapeDtypeStruct((tall, cols), jnp.bfloat16),
+        cost_estimate=pl.CostEstimate(
+            flops=2 * tall * cols * length,
+            bytes_accessed=2 * (tall * cols + length * (tall + cols)),
+            transcendentals=0,
+        ),
+        compiler_params=pltpu.CompilerParams(vmem_limit_bytes=18 * 2**20),
+    )(*flat_left, *flat_right)
+
+
+def angles(where, head):
+    half = head // 2
+    freq = THETA ** (-jnp.arange(half, dtype=jnp.float32) * 2.0 / head)
+    angle = where.astype(jnp.float32)[:, None] * freq[None, :]
+    cosine = jnp.cos(angle)
+    sine = jnp.sin(angle)
+    return jnp.concatenate([cosine, cosine], axis=-1), jnp.concatenate([-sine, sine], axis=-1)
+
+
+def grouped_body(
+    seqs,
+    parts,
+    tokens,
+    positions,
+    cotangent,
+    w_query,
+    w_key,
+    w_value,
+    w_out,
+    w_gate,
+    w_up,
+    w_down,
+    attn_gain,
+    mlp_gain,
+    query_gain,
+    key_gain,
+):
+    rows = tokens.shape[1]
+    own = w_query.shape[0]
+    group = HEADS // KV_HEADS
+    length = rows * parts
+    low = jnp.bfloat16
+    unit = w_gate.shape[1] // (seqs * parts)
+    wide = seqs * unit
+    reach = parts // 2
+    part = lax.axis_index("ctx")
+    here = lax.axis_index("seq")
+    small = query_gain.shape[0]
+
+    ring = list(range(0, parts, 2)) + list(range(parts - 1, 0, -2))
+    onward = [(ring[k], ring[(k + 1) % parts]) for k in range(parts)]
+    backward = [(b, a) for a, b in onward]
+
+    def right(value):
+        return lax.ppermute(value, "ctx", onward)
+
+    def left(value):
+        return lax.ppermute(value, "ctx", backward)
+
+    spot = jnp.where(part & 1 == 0, part >> 1, parts - ((part + 1) >> 1))
+    begin = {}
+    for step in range(1 - reach, reach + 1):
+        ahead = (spot + (parts + step)) & (parts - 1)
+        begin[step] = jnp.where(ahead < reach, 2 * ahead, 2 * (parts - ahead) - 1) * rows
+
+    def hold(values, others):
+        return lax.optimization_barrier((values, others))[0]
+
+    done = {}
+
+    def step_out(sent, jobs):
+        sent = hold(sent, ())
+        got = [(right(ahead), left(behind)) for ahead, behind in sent]
+        job = jobs.pop(0) if jobs else None
+        got, made = hold((got, () if job is None else job(sent)), ())
+        if isinstance(made, dict):
+            done.update(made)
+        return got
+
+    def ring_pieces(value, jobs=()):
+        jobs = list(jobs)
+        half = rows // 2
+        pieces = [(value,)]
+        ahead = behind = value
+        for step in range(1, reach + 1):
+            if step == reach:
+                ahead, behind = ahead[:half], behind[half:]
+            if jobs and jobs[0] is not None:
+                jobs[0] = partial(jobs[0], pieces[-1])
+            ((ahead, behind),) = step_out([(ahead, behind)], jobs)
+            pieces.append((ahead, behind))
+        return pieces
+
+    def ring_gather(value, base, jobs=()):
+        def drop(job):
+            return None if job is None else lambda piece, sent: job(sent)
+
+        pieces = ring_pieces(value, [drop(job) for job in jobs])
+        done["last"] = pieces[-1]
+        return whole_of(pieces, base)
+
+    def whole_of(pieces, base):
+        put = partial(lax.dynamic_update_slice_in_dim, axis=0, allow_negative_indices=False)
+        whole = put(base, pieces[0][0], begin[0])
+        for step in range(1, reach):
+            whole = put(put(whole, pieces[step][0], begin[-step]), pieces[step][1], begin[step])
+        whole = put(whole, pieces[reach][0], begin[reach])
+        return put(whole, pieces[reach][1], begin[reach] + rows // 2)
+
+    def ring_scatter(rings, jobs=()):
+        jobs = list(jobs)
+        half = rows // 2
+        wider = jnp.float32
+
+        def widen(pair):
+            return pair[0].astype(wider), pair[1].astype(wider)
+
+        got = step_out([(terms[reach][:half], terms[reach][half:]) for terms in rings], jobs)
+        got = [
+            (jnp.pad(ahead, ((0, half), (0, 0))), jnp.pad(behind, ((half, 0), (0, 0))))
+            for ahead, behind in map(widen, got)
+        ]
+        for step in range(reach - 1, 0, -1):
+            sent = [
+                (
+                    (terms[step][rows:].astype(wider) + ahead).astype(low),
+                    (terms[step][:rows].astype(wider) + behind).astype(low),
+                )
+                for terms, (ahead, behind) in zip(rings, got)
+            ]
+            got = [widen(pair) for pair in step_out(sent, jobs)]
+        return [
+            terms[0].astype(wider) + ahead + behind for terms, (ahead, behind) in zip(rings, got)
+        ]
+
+    def ring_terms(value):
+        def cut(step):
+            return lax.dynamic_slice_in_dim(
+                value, begin[step], rows, 0, allow_negative_indices=False
+            ).astype(low)
+
+        pairs = [jnp.concatenate([cut(-step), cut(step)]) for step in range(1, reach)]
+        return [cut(0)] + pairs + [cut(reach)]
+
+    def seq_gather(value):
+        return lax.all_gather(value, "seq", axis=0, tiled=True)
+
+    def seq_scatter(value):
+        return lax.psum_scatter(value.astype(low), "seq", scatter_dimension=0, tiled=True)
+
+    def cross(value, bit):
+        return lax.ppermute(value, "seq", [(s, s ^ bit) for s in range(seqs)])
+
+    def seq_scatter_near(value):
+        size = value.shape[0] // seqs
+
+        def cut(bits):
+            return lax.dynamic_slice_in_dim(
+                value, (here ^ bits) * size, size, 0, allow_negative_indices=False
+            ).astype(low)
+
+        far = cross(cut(3), 1).astype(jnp.float32)
+        near = cross(cut(1), 1).astype(jnp.float32)
+        other = cross((cut(2) + far).astype(low), 2).astype(jnp.float32)
+        return cut(0) + near + other
+
+    def turn(value):
+        return lax.all_to_all(value, "ctx", split_axis=0, concat_axis=0, tiled=True)
+
+    def swap_rows(value, back=False):
+        pairs = [
+            (a, (a % seqs) * parts + head_order(parts).index(a // seqs))
+            for a in range(seqs * parts)
+        ]
+        if back:
+            pairs = [(b, a) for a, b in pairs]
+        return lax.ppermute(value, ("seq", "ctx"), pairs)
+
+    my_x = tokens[0].astype(jnp.float32)
+    upstream = cotangent[0]
+    wide_q = group * HEAD_DIM
+    wide_qkv = wide_q + 2 * HEAD_DIM
+    tall = own + PAD
+    packed = fold_qkv(
+        w_query,
+        w_key,
+        w_value,
+        jnp.concatenate([attn_gain, mlp_gain, query_gain, key_gain])[None],
+        positions,
+        parts,
+    )
+
+    def pack_first(sent):
+        return packed
+
+    def pack_second(sent):
+        done["turned"] = turn(hold(packed, sent))
+        done["folded"] = fold_ff(*hold((w_gate, w_up), sent), seqs, parts)
+        return done["folded"]
+
+    def pack_third(sent):
+        done["turned"] = hold(done["turned"], sent)
+        return ()
+
+    def angle_part(sent):
+        digits = done["turned"][:, own + 1, : 2 * rows].astype(jnp.float32)
+        where = digits[:, :rows] * DIGIT + digits[:, rows:]
+        done["where"] = hold(where.astype(jnp.int32).reshape(-1), sent)
+        done["angles"] = angles(done["where"], HEAD_DIM)
+        return done["angles"]
+
+    full_x = ring_gather(
+        tokens[0],
+        jnp.zeros((length, tokens.shape[2]), low),
+        [pack_first, pack_second, pack_third, angle_part],
+    )
+    turned = done["turned"]
+    gathered = seq_gather(turned.reshape(parts * tall, wide_qkv)).reshape(-1, tall, wide_qkv)
+    gains = gathered[:, own, : 2 * (own + small)].astype(jnp.float32)
+    gain_attn = gains[:, :own].reshape(-1)
+    gain_mlp = gains[:, own : 2 * own].reshape(-1)
+    gain_query = gains[:, 2 * own : 2 * own + small].reshape(1, -1)
+    gain_key = gains[:, 2 * own + small :].reshape(1, -1)
+    start = (jnp.arange(length, dtype=jnp.int32) - done["where"])[:, None]
+    cosine, sine = done["angles"]
+
+    turned_gu = turn(hold(done["folded"], done["last"])).reshape(own * parts, -1)
+    w_d = seq_gather(w_down)
+
+    def first_part(sent):
+        full, _ = hold((full_x, gathered), sent)
+        done["first"] = project(
+            full, gathered, gain_attn[None], cosine, sine, gain_query, gain_key, own
+        )
+        done["swapped"] = swap_rows(hold(w_out, sent))
+        return done["first"], done["swapped"]
+
+    def second_part(sent):
+        _, _, query, key, value, _ = hold(done["first"], sent)
+        done["w_out"] = seq_gather(hold(done["swapped"], sent))
+        done["second"] = attend(query, key, value, start)
+        return done["second"]
+
+    def drop(job):
+        return lambda piece, sent: job(sent)
+
+    pieces_c = ring_pieces(hold(upstream, done["last"]), [drop(first_part), drop(second_part)])
+    low_one, raw, query_low, key_low, value_low, w_qkv = done["first"]
+    heads_low, lse = done["second"]
+    w_o = done["w_out"]
+    turned_gu, heads_low = hold((turned_gu, heads_low), (pieces_c[reach], w_d))
+    w_gu = seq_gather(turned_gu)
+    (summed,) = ring_scatter([ring_terms(product(hold(heads_low, turned_gu), w_o))])
+    resid = my_x + summed
+
+    normed_two, pull_two = jax.vjp(root_norm, resid, gain_mlp)
+    fed = []
+
+    def feed_next(piece, sent=()):
+        fed.append(feed(hold(piece, sent), pieces_c[len(fed)], w_gu, w_d))
+        return fed[-1]
+
+    pieces_two = ring_pieces(normed_two.astype(low), [feed_next] * reach)
+    feed_next(pieces_two[reach])
+    hidden, grad_gate_act, grad_up_act, part_out, part_two = zip(*fed)
+
+    def singly(items):
+        return [(item,) for item in items]
+
+    def sum_gu(sent):
+        return {
+            "gu": outer_sum(
+                hold(pieces_two, sent), [singly(grad_gate_act), singly(grad_up_act)], 256
+            )
+        }
+
+    def sum_down(sent):
+        done["down"] = outer_sum(singly(hold(hidden, sent)), [pieces_c], 256)
+        return done["down"]
+
+    grad_normed_two, summed = ring_scatter([part_two, part_out], [sum_down, sum_gu])
+    done["gu"] = seq_scatter(done["gu"])
+    resid_part, part_mlp = pull_two(grad_normed_two)
+    block_out = (resid + summed).astype(low)
+    grad_resid = upstream.astype(jnp.float32) + resid_part
+    heads_back = []
+
+    def back_heads(piece, sent):
+        heads_back.append(
+            [product_right(item, w_o).astype(low) for item in hold(piece, sent)]
+        )
+        return heads_back[-1]
+
+    def spread_down(piece, sent):
+        done["down"] = seq_scatter_near(hold(done["down"], sent))
+        return back_heads(piece, sent)
+
+    def end_down(piece, sent):
+        done["sent"] = sent
+        return back_heads(piece, sent), done["down"]
+
+    pieces_resid = ring_pieces(
+        grad_resid.astype(low), [spread_down, back_heads, back_heads, end_down]
+    )
+    turned_grad = turn(hold(done["gu"], done["sent"]).reshape(parts, own, 2 * wide))
+    back_heads(pieces_resid[reach], ())
+    grad_heads = whole_of(heads_back, jnp.zeros((length, wide_q), low))
+    done["back"] = attend_back(
+        query_low,
+        key_low,
+        value_low,
+        start,
+        lse,
+        grad_heads,
+        raw,
+        cosine,
+        sine,
+        gain_query,
+        gain_key,
+    )
+    qkv_back, part_query, part_key = done["back"]
+    part_normed_one = product_right(qkv_back, w_qkv)
+    _, pull_gain = jax.vjp(
+        lambda gain: root_norm(full_x.astype(jnp.float32), gain), gain_attn
+    )
+
+    def sum_qkv(sent):
+        held = hold(qkv_back, sent)
+        done["qkv"] = pack_grads(
+            low_one,
+            held,
+            pull_gain(part_normed_one)[0][None],
+            part_mlp[None],
+            part_query,
+            part_key,
+            own,
+        )
+        pieces = [
+            [lax.dynamic_slice_in_dim(heads_low, begin[0], rows, 0, allow_negative_indices=False)]
+        ]
+        half = rows // 2
+        for step in range(1, reach + 1):
+            size = rows if step < reach else half
+            pieces.append(
+                [
+                    lax.dynamic_slice_in_dim(
+                        heads_low, at, size, 0, allow_negative_indices=False
+                    )
+                    for at in (
+                        (begin[-step], begin[step])
+                        if step < reach
+                        else (begin[reach], begin[reach] + half)
+                    )
+                ]
+            )
+        done["out"] = outer_sum(pieces, [hold(pieces_resid, sent)], wide_q)
+        done["turned"] = hold(turned_grad, sent)
+        return done["qkv"], done["out"], done["turned"]
+
+    def end_gu(sent):
+        done["gu"] = unfold_ff(hold(done["turned"], sent), seqs, parts)
+        return done["gu"]
+
+    (grad_normed_one,) = ring_scatter([ring_terms(part_normed_one)], [sum_qkv, end_gu])
+    grad_gate, grad_up = done["gu"]
+    grad_down = done["down"]
+    summed = seq_scatter_near(done["qkv"]).astype(low)
+    grad_query, grad_key, grad_value, gain_sums = unfold_qkv(
+        turn(summed.reshape(parts, tall, wide_qkv)), own
+    )
+    gain_sums = gain_sums[0]
+    grad_out = swap_rows(seq_scatter(done["out"]), back=True).astype(jnp.float32)
+    _, pull_mine = jax.vjp(lambda value: root_norm(value, gain_attn), my_x)
+    grad_tokens = grad_resid + pull_mine(grad_normed_one)[0]
+    return (
+        block_out[None],
+        grad_tokens[None],
+        grad_query,
+        grad_key,
+        grad_value,
+        grad_out,
+        grad_gate,
+        grad_up,
+        grad_down,
+        gain_sums[:own],
+        gain_sums[own : 2 * own],
+        gain_sums[2 * own : 2 * own + small],
+        gain_sums[2 * own + small : 2 * (own + small)],
+    )
+
+
 def solution(mesh):
+    grouped = mesh.shape["ctx"] == KV_HEADS and mesh.shape["seq"] == 4
     return jax.shard_map(
-        body,
+        partial(grouped_body, mesh.shape["seq"], mesh.shape["ctx"]) if grouped else whole_body,
         mesh=mesh,
         in_specs=(
             P("seq", "ctx", None),

time: 3530 us -> 546 us (0.15)
  waiting for transfers between devices: 3130 us -> 224 us
  matrix products: 235 us -> 12.5 us
  starting transfers between devices: 0.9 us -> 115 us
  blocking collectives: 88.3 us -> 0 us
  Pallas kernels: 0 us -> 78.5 us
    reduce_scatter x9 -> x2, waiting for transfers between devices: 2400 us -> 0.01 us  [seq_scatter(): lax.psum_scatter(value.astype(low), 'seq', scatter_dimension=0, tiled=True)]
    all_gather x9 -> x4, waiting for transfers between devices: 729 us -> 0.02 us  [seq_gather(): return lax.all_gather(value, 'seq', axis=0, tiled=True)]
    ppermute x0 -> x72, waiting for transfers between devices: none -> 220 us  [the longest x32 171 us: right(): return lax.ppermute(value, 'ctx', onward)]
    dot_general x13 -> x0, matrix products: 117 us -> none  [the longest x7 91 us: product_left(): lax.dot_general(left, right, (((0,), (0,)), ((), ())), preferred_element_...]
    ppermute x0 -> x72, starting transfers between devices: none -> 92.3 us  [the longest x32 54.3 us: right(): return lax.ppermute(value, 'ctx', onward)]
    unnamed x2 -> x0, blocking collectives: 88.3 us -> none
    pallas_call x0 -> x16, Pallas kernels: none -> 78.5 us  [the longest x5 28 us: feed(): pl.pallas_call(partial(feed_kernel, count), out_shape=[jax.ShapeDtypeStru...]
    dot_general x7 -> x1, matrix products: 55.7 us -> 2.49 us  [product(): return jnp.dot(left, right, preferred_element_type=jnp.float32)]
  transfers between devices with their start and end apart: 18 -> 82, of which waited for: 18 -> 51; matrix products, arithmetic and copies ran while one was open for 6% -> 12% of each run, Pallas kernels for 0% -> 14%
where the time goes in v1:
time: 546 us; the launch traced here: 536 us
  waiting for transfers between devices  224 us (41%)
  starting transfers between devices  115 us (21%)
  Pallas kernels  78.5 us (14%)
  local copies, waits for them, and re-layouts  50 us (9%)
  other arithmetic  41.3 us (8%)
  between operations  15.8 us (3%)
  matrix products  12.5 us (2%)
    ppermute x32, waiting for transfers between devices, right(): return lax.ppermute(value, 'ctx', onward)  171 us
    ppermute x32, starting transfers between devices, right(): return lax.ppermute(value, 'ctx', onward)  54.3 us
    ppermute x32, waiting for transfers between devices, left(): return lax.ppermute(value, 'ctx', backward)  42.4 us
    unnamed x162, local copies, waits for them, and re-layouts  32.9 us
    pallas_call x5, Pallas kernels, feed(): pl.pallas_call(partial(feed_kernel, count), out_shape=[jax.ShapeDtypeStru...  28 us
    ppermute x32, starting transfers between devices, left(): return lax.ppermute(value, 'ctx', backward)  26.6 us
    all_to_all x4, starting transfers between devices, turn(): return lax.all_to_all(value, 'ctx', split_axis=0, concat_axis=0, tiled=True)  21.6 us
    pallas_call x3, Pallas kernels, outer_sum(): pl.pallas_call(partial(outer_kernel, [len(group) for group in lefts], [[l...  19.4 us
  transfers between devices with their start and end apart: 82, of which 51 were waited for; matrix products, arithmetic and copies ran while one was open for 12% of the time, Pallas kernels for 14%

profile of v1, /device:TPU:0, one launch (start us, length us, event | category | flops | bytes accessed | tf_op | source)
XLA Modules:
  0.0 536.4 jit_solution(8572606807203552491)
XLA Ops:
  7.2 3.1 collective-permute-start
  13.6 8.7 %collective-permute-done = bf16[128,2048]{1,0:T(8,128)(2,1)S(1)} collective-permute-done((bf16[128,2048]{1,0:T(8,128)(2,1)}, bf16[128,2048]{1,0:T(8,128)(2,1)S(1)}, u32[]{:S(2)}, u32[]{:S(2)}) %collective-permute-start) | collective-permute-done | bytes 524320 | tf_op jit(solution)/shard_map/ppermute | solution.py:763
  23.9 4.8 all-to-all-start
  30.8 2.8 shard_map.238
  33.6 15.9 %collective-permute-done.2 = bf16[128,2048]{1,0:T(8,128)(2,1)S(1)} collective-permute-done((bf16[128,2048]{1,0:T(8,128)(2,1)S(1)}, bf16[128,2048]{1,0:T(8,128)(2,1)S(1)}, u32[]{:S(2)}, u32[]{:S(2)}) %collective-permute-start.2) | collective-permute-done | bytes 524320 | tf_op jit(solution)/shard_map/ppermute | solution.py:763
  53.3 2.5 broadcast_in_dim.32
  57.5 5.0 collective-permute-start.4
  65.0 7.0 %collective-permute-done.4 = bf16[128,2048]{1,0:T(8,128)(2,1)S(1)} collective-permute-done((bf16[128,2048]{1,0:T(8,128)(2,1)S(1)}, bf16[128,2048]{1,0:T(8,128)(2,1)S(1)}, u32[]{:S(2)}, u32[]{:S(2)}) %collective-permute-start.4) | collective-permute-done | bytes 524320 | tf_op jit(solution)/shard_map/ppermute | solution.py:763
  81.8 4.3 all-to-all-start.1
  94.8 6.2 %shard_map.239 = (bf16[1024,2048]{1,0:T(8,128)(2,1)S(1)}, f32[1024,384]{1,0:T(8,128)S(1)}, bf16[1024,256]{1,0:T(8,128)(2,1)S(1)}, bf16[1024,128]{1,0:T(8,128)(2,...) custom-call(bf16[1024,2048]{1,0:T(8,128)(2,1)} %constant_dynamic-update-slice_fusion.7.tokens, ...), custom_call_target="tpu_custom_call" | custom-call | flops 2147483648 | bytes 14000000 | tf_op jit(solution)/shard_map/pallas_call | solution.py:435
  107.1 13.7 %collective-permute-done.8.refs_2_.refs_6_ = bf16[128,2048]{1,0:T(8,128)(2,1)S(1)} collective-permute-done((bf16[128,2048]{1,0:T(8,128)(2,1)S(1)}, bf16[128,2048]{1,0:T(8,128)(2,1)S(1)}, u32[]{:S(2)}, u32[]{:S(2)}) %collective-permute-start.8) | collective-permute-done | bytes 524320 | tf_op jit(solution)/shard_map/ppermute | solution.py:763
  120.8 4.7 collective-permute-done.9.refs_3_.refs_7_
  125.5 7.4 %collective-permute-start.11 = (bf16[128,2048]{1,0:T(8,128)(2,1)S(1)}, bf16[128,2048]{1,0:T(8,128)(2,1)S(1)}, u32[]{:S(2)}, u32[]{:S(2)}) collective-permute-start(bf16[128,2048]{1,0:T(8,128)(2,1)S(1)} %collective-permute-done.8.refs_2_.refs_6_), channel_id=1, source_target_pairs={{0,2},{2,4},{4,6},{6,7},{7,5},{5,3},{3,1},{1,0},{8,10},{10,12},{12... | collective-permute-start | bytes 1572872 | tf_op jit(solution)/shard_map/ppermute | solution.py:763
  135.1 4.5 shard_map.240
  140.4 4.3 collective-permute-done.11.refs_2_.refs_8_
  149.8 10.3 %collective-permute-done.13.refs_2_.refs_10_ = bf16[128,2048]{1,0:T(8,128)(2,1)S(1)} collective-permute-done((bf16[128,2048]{1,0:T(8,128)(2,1)S(1)}, bf16[128,2048]{1,0:T(8,128)(2,1)S(1)}, u32[]{:S(2)}, u32[]{:S(2)}) %collective-permute-start.13) | collective-permute-done | bytes 524320 | tf_op jit(solution)/shard_map/ppermute | solution.py:763
  164.8 4.8 collective-permute-done.15.refs_2_.refs_12_
  171.3 2.5 fusion.24
  176.0 4.5 collective-permute-done.17
  184.0 8.3 %collective-permute-done.19 = bf16[128,2048]{1,0:T(8,128)(2,1)S(1)} collective-permute-done((bf16[128,2048]{1,0:T(8,128)(2,1)S(1)}, bf16[128,2048]{1,0:T(8,128)(2,1)S(1)}, u32[]{:S(2)}, u32[]{:S(2)}) %collective-permute-start.19) | collective-permute-done | bytes 524320 | tf_op jit(solution)/shard_map/ppermute | solution.py:763
  196.0 7.8 %collective-permute-done.21 = bf16[128,2048]{1,0:T(8,128)(2,1)S(1)} collective-permute-done((bf16[128,2048]{1,0:T(8,128)(2,1)S(1)}, bf16[128,2048]{1,0:T(8,128)(2,1)S(1)}, u32[]{:S(2)}, u32[]{:S(2)}) %collective-permute-start.21) | collective-permute-done | bytes 524320 | tf_op jit(solution)/shard_map/ppermute | solution.py:763
  208.2 7.4 %collective-permute-done.23 = bf16[128,2048]{1,0:T(8,128)(2,1)} collective-permute-done((bf16[128,2048]{1,0:T(8,128)(2,1)}, bf16[128,2048]{1,0:T(8,128)(2,1)}, u32[]{:S(2)}, u32[]{:S(2)}) %collective-permute-start.23) | collective-permute-done | bytes 524320 | tf_op jit(solution)/shard_map/ppermute | solution.py:763
  221.9 2.8 copy-done
  225.7 5.6 %shard_map.241 = (bf16[128,768]{1,0:T(8,128)(2,1)S(1)}, bf16[128,768]{1,0:T(8,128)(2,1)S(1)}, bf16[128,768]{1,0:T(8,128)(2,1)S(1)}, bf16[128,2048]{1,0:T(8,128)(2,1)S(1)}, bf16[128,2048]{1,0:T(8,128)(2,1)S(1)}) custom-call(bf16[128,2048]{1,0:T(8,128)(2,1)} %multiply_convert_fusion.refs_0_, bf16[128,2048]{1,0:T(8,128)(2,1)S(1)} %bitcast.68, ...), custom_call_target="tpu_custom_call" | custom-call | flops 2415919104 | bytes 12582912 | tf_op jit(solution)/shard_map/pallas_call | solution.py:661
  235.0 6.4 %shard_map.242 = (bf16[256,768]{1,0:T(8,128)(2,1)S(1)}, bf16[256,768]{1,0:T(8,128)(2,1)S(1)}, bf16[256,768]{1,0:T(8,128)(2,1)S(1)}, bf16[256,2048]{1,0:T(8,128)(2,1)S(1)}, bf16[256,2048]{1,0:T(8,128)(2,1)S(1)}) custom-call(bf16[128,2048]{1,0:T(8,128)(2,1)} %collective-permute-done.25.refs_0_.refs_1_, ...), custom_call_target="tpu_custom_call" | custom-call | flops 4831838208 | bytes 15728640 | tf_op jit(solution)/shard_map/pallas_call | solution.py:661
  243.4 2.7 collective-permute-done.27.refs_0_.refs_3_
  248.6 6.3 %shard_map.243 = (bf16[256,768]{1,0:T(8,128)(2,1)S(1)}, bf16[256,768]{1,0:T(8,128)(2,1)S(1)}, bf16[256,768]{1,0:T(8,128)(2,1)S(1)}, bf16[256,2048]{1,0:T(8,128)(2,1)S(1)}, bf16[256,2048]{1,0:T(8,128)(2,1)S(1)}) custom-call(bf16[128,2048]{1,0:T(8,128)(2,1)S(1)} %collective-permute-done.27.refs_0_.refs_3_, ...), custom_call_target="tpu_custom_call" | custom-call | flops 4831838208 | bytes 15728640 | tf_op jit(solution)/shard_map/pallas_call | solution.py:661
  260.8 5.2 shard_map.244
  267.0 4.4 shard_map.245
  273.9 2.9 collective-permute-start.35
  276.9 5.8 %shard_map.246 = bf16[768,2048]{1,0:T(8,128)(2,1)S(1)} custom-call(bf16[128,768]{1,0:T(8,128)(2,1)S(1)} %get-tuple-element.370.refs_0_, bf16[256,768]{1,0:T(8,128)(2,1)S(1)} %get-tuple-element.371.refs_1_, bf16[256,768]{1,0:T(8,128)(2,1)S(1)} %get-tuple-element.372.refs_2_, bf16[256,768]{1,0:T(8,128)(2,1)S(1)} %get-tuple-element.373.refs_3_, ...), custom_call_target="tpu_custom_call" | custom-call | flops 3221225472 | bytes 8912896 | tf_op jit(solution)/shard_map/pallas_call | solution.py:699
  283.8 2.5 collective-permute-done.35
  286.4 3.1 collective-permute-done.36
  294.0 11.1 %shard_map.247 = bf16[2048,1536]{1,0:T(8,128)(2,1)S(1)} custom-call(bf16[128,2048]{1,0:T(8,128)(2,1)} %multiply_convert_fusion.refs_0_, bf16[128,2048]{1,0:T(8,128)(2,1)} %collective-permute-done.25.refs_0_.refs_1_, bf16[128,2048]{1,0:T(8,128)(2,1)} %collective-permute-done.26.refs_1_.refs_2_, bf16[128,2048]{1,0:T(8,128)(2,1)S(1)} %collective-permute-done.27.refs_0_.refs_3_, ...), custom_call_target="tpu_custom_call" | custom-call | flops 6442450944 | bytes 13631488 | tf_op jit(solution)/shard_map/pallas_call | solution.py:699
  305.2 2.7 copy-done.2
  310.1 3.0 add_convert_fusion.14
  313.1 2.6 add_convert_fusion.16
  315.7 2.5 collective-permute-start.41
  320.2 7.8 %collective-permute-done.41 = bf16[128,2048]{1,0:T(8,128)(2,1)S(1)} collective-permute-done((bf16[128,2048]{1,0:T(8,128)(2,1)}, bf16[128,2048]{1,0:T(8,128)(2,1)S(1)}, u32[]{:S(2)}, u32[]{:S(2)}) %collective-permute-start.41) | collective-permute-done | bytes 524320 | tf_op jit(solution)/shard_map/ppermute | solution.py:763
  328.0 2.7 collective-permute-done.42
  330.6 8.6 %collective-permute-done.43 = bf16[128,2048]{1,0:T(8,128)(2,1)} collective-permute-done((bf16[128,2048]{1,0:T(8,128)(2,1)}, bf16[128,2048]{1,0:T(8,128)(2,1)}, u32[]{:S(2)}, u32[]{:S(2)}) %collective-permute-start.43) | collective-permute-done | bytes 524320 | tf_op jit(solution)/shard_map/ppermute | solution.py:763
  339.2 2.8 collective-permute-done.44
  348.1 3.1 fusion
  351.2 5.5 %collective-permute-done.45 = bf16[128,2048]{1,0:T(8,128)(2,1)S(1)} collective-permute-done((bf16[128,2048]{1,0:T(8,128)(2,1)S(1)}, bf16[128,2048]{1,0:T(8,128)(2,1)S(1)}, u32[]{:S(2)}, u32[]{:S(2)}) %collective-permute-start.45) | collective-permute-done | bytes 524320 | tf_op jit(solution)/shard_map/ppermute | solution.py:763
  357.7 6.8 %collective-permute-done.47 = bf16[128,2048]{1,0:T(8,128)(2,1)S(1)} collective-permute-done((bf16[128,2048]{1,0:T(8,128)(2,1)S(1)}, bf16[128,2048]{1,0:T(8,128)(2,1)S(1)}, u32[]{:S(2)}, u32[]{:S(2)}) %collective-permute-start.47) | collective-permute-done | bytes 524320 | tf_op jit(solution)/shard_map/ppermute | solution.py:763
  371.0 9.0 %collective-permute-done.49.refs_10_ = bf16[128,2048]{1,0:T(8,128)(2,1)S(1)} collective-permute-done((bf16[128,2048]{1,0:T(8,128)(2,1)S(1)}, bf16[128,2048]{1,0:T(8,128)(2,1)S(1)}, u32[]{:S(2)}, u32[]{:S(2)}) %collective-permute-start.49) | collective-permute-done | bytes 524320 | tf_op jit(solution)/shard_map/ppermute | solution.py:763
  385.7 7.9 %collective-permute-done.51.refs_12_ = bf16[128,2048]{1,0:T(8,128)(2,1)S(1)} collective-permute-done((bf16[128,2048]{1,0:T(8,128)(2,1)S(1)}, bf16[128,2048]{1,0:T(8,128)(2,1)S(1)}, u32[]{:S(2)}, u32[]{:S(2)}) %collective-permute-start.51) | collective-permute-done | bytes 524320 | tf_op jit(solution)/shard_map/ppermute | solution.py:763
  397.1 8.9 %collective-permute-done.53.refs_14_ = bf16[128,2048]{1,0:T(8,128)(2,1)S(1)} collective-permute-done((bf16[128,2048]{1,0:T(8,128)(2,1)S(1)}, bf16[128,2048]{1,0:T(8,128)(2,1)S(1)}, u32[]{:S(2)}, u32[]{:S(2)}) %collective-permute-start.53) | collective-permute-done | bytes 524320 | tf_op jit(solution)/shard_map/ppermute | solution.py:763
  414.8 7.6 %shard_map.248 = (bf16[1024,512]{1,0:T(8,128)(2,1)S(1)}, f32[1,128]{1,0:T(1,128)S(1)}, f32[1,128]{1,0:T(1,128)S(1)}) custom-call(bf16[1024,256]{1,0:T(8,128)(2,1)S(1)} %copy-done.57, bf16[1024,128]{1,0:T(8,128)(2,1)S(1)} %copy-done.59, bf16[1024,128]{1,0:T(8,128)(2,1)S(1)} %copy-done.62, s32[1024,1]{1,0:T(8,128)S(1)} %copy-done.34, ...), custom_call_target="tpu_custom_call" | custom-call | flops 2684354560 | bytes 6000000 | tf_op jit(solution)/shard_map/pallas_call | solution.py:576
  423.4 6.7 %all-to-all-start.2 = ((bf16[8,64,1536]{2,1,0:T(8,128)(2,1)}), bf16[8,64,1536]{2,1,0:T(8,128)(2,1)}, u32[]{:S(2)}, u32[]{:S(2)}) async-start(bf16[8,64,1536]{2,1,0:T(8,128)(2,1)} %bitcast.77), calls=%async_computation.3 | async-start | bytes 3145728 | tf_op jit(solution)/shard_map/all_to_all | solution.py:876
  430.5 5.7 %fusion.2 = (f32[2048]{0:T(1024)S(1)}, bf16[1024,2048]{1,0:T(8,128)(2,1)S(1)}) fusion(bf16[1024,2048]{1,0:T(8,128)(2,1)} %constant_dynamic-update-slice_fusion.7.tokens, f32[1024]{0:T(1024)S(1)} %add_rsqrt_fusion, bf16[1024,512]{1,0:T(8,128)(2,1)} %copy-done.53, bf16[2048,512]{1,0:T(8,128)(2,1)} %copy-done.50), kind=kOutput, calls=%fused_computation.4 | convolution fusion | flops 2157967360 | bytes 11546624 | tf_op jit(solution)/shard_map/dot_general | solution.py:56
  447.8 2.5 shard_map.250
  451.8 5.1 collective-permute-start.70
  456.9 3.4 all-to-all-done.2.turned
  462.6 3.5 collective-permute-start.62
  466.1 6.1 %collective-permute-done.70 = bf16[640,512]{1,0:T(8,128)(2,1)S(1)} collective-permute-done((bf16[640,512]{1,0:T(8,128)(2,1)S(1)}, bf16[640,512]{1,0:T(8,128)(2,1)S(1)}, u32[]{:S(2)}, u32[]{:S(2)}) %collective-permute-start.70) | collective-permute-done | bytes 655392 | tf_op jit(solution)/shard_map/ppermute | solution.py:860
  474.4 5.8 %all-to-all-start.3 = ((bf16[8,80,512]{2,1,0:T(8,128)(2,1)}), bf16[8,80,512]{2,1,0:T(8,128)(2,1)S(1)}, u32[]{:S(2)}, u32[]{:S(2)}) async-start(bf16[8,80,512]{2,1,0:T(8,128)(2,1)} %bitcast.13), calls=%async_computation.4 | async-start | bytes 1310720 | tf_op jit(solution)/shard_map/all_to_all | solution.py:876
  480.3 3.5 shard_map.251
  483.8 2.8 add_convert_fusion.5
  490.2 12.5 %collective-permute-done.64 = bf16[128,2048]{1,0:T(8,128)(2,1)S(1)} collective-permute-done((bf16[128,2048]{1,0:T(8,128)(2,1)}, bf16[128,2048]{1,0:T(8,128)(2,1)S(1)}, u32[]{:S(2)}, u32[]{:S(2)}) %collective-permute-start.64) | collective-permute-done | bytes 524320 | tf_op jit(solution)/shard_map/ppermute | solution.py:763
  502.7 3.7 collective-permute-done.65
  506.4 2.8 add_convert_fusion.3
  509.2 3.3 collective-permute-start.66
  519.5 3.5 collective-permute-done.66
  (372 shorter events, 169.3 us)
Async XLA Ops:
  7.2 15.1 %collective-permute-start = (bf16[128,2048]{1,0:T(8,128)(2,1)}, bf16[128,2048]{1,0:T(8,128)(2,1)S(1)}, u32[]{:S(2)}, u32[]{:S(2)}) collective-permute-start(bf16[128,2048]{1,0:T(8,128)(2,1)} %bitcast.74), channel_id=1, source_target_pairs={{0,2},{2,4},{4,6},{6,7},{7,5},{5,3},{3,1},{1,0},{8,10},{10,12},{12... | collective-permute-start | bytes 1572872 | tf_op jit(solution)/shard_map/ppermute | solution.py:763
  10.3 13.6 %collective-permute-start.1 = (bf16[128,2048]{1,0:T(8,128)(2,1)}, bf16[128,2048]{1,0:T(8,128)(2,1)S(1)}, u32[]{:S(2)}, u32[]{:S(2)}) collective-permute-start(bf16[128,2048]{1,0:T(8,128)(2,1)} %bitcast.75), channel_id=1, source_target_pairs={{2,0},{4,2},{6,4},{7,6},{5,7},{3,5},{1,3},{0,1},{10,8},{12,10},{14... | collective-permute-start | bytes 1572872 | tf_op jit(solution)/shard_map/ppermute | solution.py:766
  23.9 27.8 %all-to-all-start = ((bf16[8,80,512]{2,1,0:T(8,128)(2,1)}), bf16[8,80,512]{2,1,0:T(8,128)(2,1)S(1)}, u32[]{:S(2)}, u32[]{:S(2)}) async-start(bf16[8,80,512]{2,1,0:T(8,128)(2,1)} %shard_map.237), calls=%async_computation | async-start | bytes 1310720 | tf_op jit(solution)/shard_map/all_to_all | solution.py:876
  28.6 62.7 %all-gather.5.cloned.1.call-start = ((), (), s32[]{:S(2)}) async-start(), calls=%async_computation.6 | async-start | bytes 3276800 | tf_op jit(solution)/shard_map/all_gather | solution.py:854
  28.7 20.8 %collective-permute-start.2 = (bf16[128,2048]{1,0:T(8,128)(2,1)S(1)}, bf16[128,2048]{1,0:T(8,128)(2,1)S(1)}, u32[]{:S(2)}, u32[]{:S(2)}) collective-permute-start(bf16[128,2048]{1,0:T(8,128)(2,1)S(1)} %collective-permute-done), channel_id=1, source_target_pairs={{0,2},{2,4},{4,6},{6,7},{7,5},{5,3},{3,1},{1,0},{8,10},{10,12},{12... | collective-permute-start | bytes 1572872 | tf_op jit(solution)/shard_map/ppermute | solution.py:763
  30.7 20.9 %collective-permute-start.3 = (bf16[128,2048]{1,0:T(8,128)(2,1)S(1)}, bf16[128,2048]{1,0:T(8,128)(2,1)S(1)}, u32[]{:S(2)}, u32[]{:S(2)}) collective-permute-start(bf16[128,2048]{1,0:T(8,128)(2,1)S(1)} %collective-permute-done.1), channel_id=1, source_target_pairs={{2,0},{4,2},{6,4},{7,6},{5,7},{3,5},{1,3},{0,1},{10,8},{12,10},{14... | collective-permute-start | bytes 1572872 | tf_op jit(solution)/shard_map/ppermute | solution.py:766
  52.5 118.5 %all-gather.7.cloned.1.call-start = ((), (), s32[]{:S(2)}) async-start(), calls=%async_computation.7 | async-start | bytes 3932160 | tf_op jit(solution)/shard_map/all_gather | solution.py:854
  57.5 14.5 %collective-permute-start.4 = (bf16[128,2048]{1,0:T(8,128)(2,1)S(1)}, bf16[128,2048]{1,0:T(8,128)(2,1)S(1)}, u32[]{:S(2)}, u32[]{:S(2)}) collective-permute-start(bf16[128,2048]{1,0:T(8,128)(2,1)S(1)} %collective-permute-done.2), channel_id=1, source_target_pairs={{0,2},{2,4},{4,6},{6,7},{7,5},{5,3},{3,1},{1,0},{8,10},{10,12},{12... | collective-permute-start | bytes 1572872 | tf_op jit(solution)/shard_map/ppermute | solution.py:763
  62.5 11.7 %collective-permute-start.5 = (bf16[128,2048]{1,0:T(8,128)(2,1)S(1)}, bf16[128,2048]{1,0:T(8,128)(2,1)S(1)}, u32[]{:S(2)}, u32[]{:S(2)}) collective-permute-start(bf16[128,2048]{1,0:T(8,128)(2,1)S(1)} %collective-permute-done.3), channel_id=1, source_target_pairs={{2,0},{4,2},{6,4},{7,6},{5,7},{3,5},{1,3},{0,1},{10,8},{12,10},{14... | collective-permute-start | bytes 1572872 | tf_op jit(solution)/shard_map/ppermute | solution.py:766
  81.8 89.2 %all-to-all-start.1 = ((bf16[8,64,1536]{2,1,0:T(8,128)(2,1)}), bf16[8,64,1536]{2,1,0:T(8,128)(2,1)}, u32[]{:S(2)}, u32[]{:S(2)}) async-start(bf16[8,64,1536]{2,1,0:T(8,128)(2,1)} %shard_map.238), calls=%async_computation.1 | async-start | bytes 3145728 | tf_op jit(solution)/shard_map/all_to_all | solution.py:876
  86.2 85.1 %all-gather.9.cloned.1.call-start = ((), (), s32[]{:S(2)}) async-start(), calls=%async_computation.8 | async-start | bytes 1310720 | tf_op jit(solution)/shard_map/all_gather | solution.py:854
  87.0 33.8 %collective-permute-start.8 = (bf16[128,2048]{1,0:T(8,128)(2,1)S(1)}, bf16[128,2048]{1,0:T(8,128)(2,1)S(1)}, u32[]{:S(2)}, u32[]{:S(2)}) collective-permute-start(bf16[128,2048]{1,0:T(8,128)(2,1)S(1)} %bitcast.66), channel_id=1, source_target_pairs={{0,2},{2,4},{4,6},{6,7},{7,5},{5,3},{3,1},{1,0},{8,10},{10,12},{12... | collective-permute-start | bytes 1572872 | tf_op jit(solution)/shard_map/ppermute | solution.py:763
  88.8 36.7 %collective-permute-start.9 = (bf16[128,2048]{1,0:T(8,128)(2,1)S(1)}, bf16[128,2048]{1,0:T(8,128)(2,1)S(1)}, u32[]{:S(2)}, u32[]{:S(2)}) collective-permute-start(bf16[128,2048]{1,0:T(8,128)(2,1)S(1)} %bitcast.67), channel_id=1, source_target_pairs={{2,0},{4,2},{6,4},{7,6},{5,7},{3,5},{1,3},{0,1},{10,8},{12,10},{14... | collective-permute-start | bytes 1572872 | tf_op jit(solution)/shard_map/ppermute | solution.py:766
  89.0 18.1 %collective-permute-start.10 = (bf16[64,2048]{1,0:T(8,128)(2,1)}, bf16[64,2048]{1,0:T(8,128)(2,1)S(1)}, u32[]{:S(2)}, u32[]{:S(2)}) collective-permute-start(bf16[64,2048]{1,0:T(8,128)(2,1)} %param.20), channel_id=1, source_target_pairs={{0,0},{1,8},{2,16},{3,24},{4,4},{5,12},{6,20},{7,28},{8,1},{9,9},{... | collective-permute-start | bytes 786440 | tf_op jit(solution)/shard_map/ppermute | solution.py:885
  125.5 96.4 %all-gather.11.cloned.1.call-start = ((), (), s32[]{:S(2)}) async-start(), calls=%async_computation.9 | async-start | bytes 7864320 | tf_op jit(solution)/shard_map/all_gather | solution.py:854
  125.5 19.1 %collective-permute-start.11 = (bf16[128,2048]{1,0:T(8,128)(2,1)S(1)}, bf16[128,2048]{1,0:T(8,128)(2,1)S(1)}, u32[]{:S(2)}, u32[]{:S(2)}) collective-permute-start(bf16[128,2048]{1,0:T(8,128)(2,1)S(1)} %collective-permute-done.8.refs_2_.refs_6_), channel_id=1, source_target_pairs={{0,2},{2,4},{4,6},{6,7},{7,5},{5,3},{3,1},{1,0},{8,10},{10,12},{12... | collective-permute-start | bytes 1572872 | tf_op jit(solution)/shard_map/ppermute | solution.py:763
  132.9 14.1 %collective-permute-start.12 = (bf16[128,2048]{1,0:T(8,128)(2,1)S(1)}, bf16[128,2048]{1,0:T(8,128)(2,1)}, u32[]{:S(2)}, u32[]{:S(2)}) collective-permute-start(bf16[128,2048]{1,0:T(8,128)(2,1)S(1)} %collective-permute-done.9.refs_3_.refs_7_), channel_id=1, source_target_pairs={{2,0},{4,2},{6,4},{7,6},{5,7},{3,5},{1,3},{0,1},{10,8},{12,10},{14... | collective-permute-start | bytes 1572872 | tf_op jit(solution)/shard_map/ppermute | solution.py:766
  147.0 13.1 %collective-permute-start.13 = (bf16[128,2048]{1,0:T(8,128)(2,1)S(1)}, bf16[128,2048]{1,0:T(8,128)(2,1)S(1)}, u32[]{:S(2)}, u32[]{:S(2)}) collective-permute-start(bf16[128,2048]{1,0:T(8,128)(2,1)S(1)} %collective-permute-done.11.refs_2_.refs_8_), channel_id=1, source_target_pairs={{0,2},{2,4},{4,6},{6,7},{7,5},{5,3},{3,1},{1,0},{8,10},{10,12},{12... | collective-permute-start | bytes 1572872 | tf_op jit(solution)/shard_map/ppermute | solution.py:763
  148.4 13.5 %collective-permute-start.14 = (bf16[128,2048]{1,0:T(8,128)(2,1)}, bf16[128,2048]{1,0:T(8,128)(2,1)S(1)}, u32[]{:S(2)}, u32[]{:S(2)}) collective-permute-start(bf16[128,2048]{1,0:T(8,128)(2,1)} %collective-permute-done.12.refs_3_.refs_9_), channel_id=1, source_target_pairs={{2,0},{4,2},{6,4},{7,6},{5,7},{3,5},{1,3},{0,1},{10,8},{12,10},{14... | collective-permute-start | bytes 1572872 | tf_op jit(solution)/shard_map/ppermute | solution.py:766
  171.0 252.4 %reduce-scatter.3.cloned.1.call-start = ((), (), s32[]{:S(2)}) async-start(), calls=%async_computation.10 | async-start | bytes 7864320 | tf_op jit(solution)/shard_map/reduce_scatter | solution.py:857
  182.3 11.2 %collective-permute-start.20 = (bf16[128,2048]{1,0:T(8,128)(2,1)S(1)}, bf16[128,2048]{1,0:T(8,128)(2,1)S(1)}, u32[]{:S(2)}, u32[]{:S(2)}) collective-permute-start(bf16[128,2048]{1,0:T(8,128)(2,1)S(1)} %get-tuple-element.307), channel_id=1, source_target_pairs={{2,0},{4,2},{6,4},{7,6},{5,7},{3,5},{1,3},{0,1},{10,8},{12,10},{14... | collective-permute-start | bytes 1572872 | tf_op jit(solution)/shard_map/ppermute | solution.py:766
  219.9 13.1 %collective-permute-start.25 = (bf16[128,2048]{1,0:T(8,128)(2,1)}, bf16[128,2048]{1,0:T(8,128)(2,1)}, u32[]{:S(2)}, u32[]{:S(2)}) collective-permute-start(bf16[128,2048]{1,0:T(8,128)(2,1)} %multiply_convert_fusion.refs_0_), channel_id=1, source_target_pairs={{0,2},{2,4},{4,6},{6,7},{7,5},{5,3},{3,1},{1,0},{8,10},{10,12},{12... | collective-permute-start | bytes 1572872 | tf_op jit(solution)/shard_map/ppermute | solution.py:763
  220.3 12.7 %collective-permute-start.26 = (bf16[128,2048]{1,0:T(8,128)(2,1)}, bf16[128,2048]{1,0:T(8,128)(2,1)}, u32[]{:S(2)}, u32[]{:S(2)}) collective-permute-start(bf16[128,2048]{1,0:T(8,128)(2,1)} %multiply_convert_fusion.refs_0_), channel_id=1, source_target_pairs={{2,0},{4,2},{6,4},{7,6},{5,7},{3,5},{1,3},{0,1},{10,8},{12,10},{14... | collective-permute-start | bytes 1572872 | tf_op jit(solution)/shard_map/ppermute | solution.py:766
  233.0 13.2 %collective-permute-start.27 = (bf16[128,2048]{1,0:T(8,128)(2,1)}, bf16[128,2048]{1,0:T(8,128)(2,1)S(1)}, u32[]{:S(2)}, u32[]{:S(2)}) collective-permute-start(bf16[128,2048]{1,0:T(8,128)(2,1)} %collective-permute-done.25.refs_0_.refs_1_), channel_id=1, source_target_pairs={{0,2},{2,4},{4,6},{6,7},{7,5},{5,3},{3,1},{1,0},{8,10},{10,12},{12... | collective-permute-start | bytes 1572872 | tf_op jit(solution)/shard_map/ppermute | solution.py:763
  233.4 12.7 %collective-permute-start.28 = (bf16[128,2048]{1,0:T(8,128)(2,1)}, bf16[128,2048]{1,0:T(8,128)(2,1)S(1)}, u32[]{:S(2)}, u32[]{:S(2)}) collective-permute-start(bf16[128,2048]{1,0:T(8,128)(2,1)} %collective-permute-done.26.refs_1_.refs_2_), channel_id=1, source_target_pairs={{2,0},{4,2},{6,4},{7,6},{5,7},{3,5},{1,3},{0,1},{10,8},{12,10},{14... | collective-permute-start | bytes 1572872 | tf_op jit(solution)/shard_map/ppermute | solution.py:766
  246.1 12.0 %collective-permute-start.29 = (bf16[128,2048]{1,0:T(8,128)(2,1)S(1)}, bf16[128,2048]{1,0:T(8,128)(2,1)S(1)}, u32[]{:S(2)}, u32[]{:S(2)}) collective-permute-start(bf16[128,2048]{1,0:T(8,128)(2,1)S(1)} %collective-permute-done.27.refs_0_.refs_3_), channel_id=1, source_target_pairs={{0,2},{2,4},{4,6},{6,7},{7,5},{5,3},{3,1},{1,0},{8,10},{10,12},{12... | collective-permute-start | bytes 1572872 | tf_op jit(solution)/shard_map/ppermute | solution.py:763
  246.2 12.4 %collective-permute-start.30 = (bf16[128,2048]{1,0:T(8,128)(2,1)S(1)}, bf16[128,2048]{1,0:T(8,128)(2,1)S(1)}, u32[]{:S(2)}, u32[]{:S(2)}) collective-permute-start(bf16[128,2048]{1,0:T(8,128)(2,1)S(1)} %collective-permute-done.28.refs_1_.refs_4_), channel_id=1, source_target_pairs={{2,0},{4,2},{6,4},{7,6},{5,7},{3,5},{1,3},{0,1},{10,8},{12,10},{14... | collective-permute-start | bytes 1572872 | tf_op jit(solution)/shard_map/ppermute | solution.py:766
  273.9 12.4 %collective-permute-start.35 = (bf16[64,2048]{1,0:T(8,128)(2,1)S(1)}, bf16[64,2048]{1,0:T(8,128)(2,1)S(1)}, u32[]{:S(2)}, u32[]{:S(2)}) collective-permute-start(bf16[64,2048]{1,0:T(8,128)(2,1)S(1)} %get-tuple-element.367), channel_id=1, source_target_pairs={{0,2},{2,4},{4,6},{6,7},{7,5},{5,3},{3,1},{1,0},{8,10},{10,12},{12... | collective-permute-start | bytes 786440 | tf_op jit(solution)/shard_map/ppermute | solution.py:763
  276.9 12.6 %collective-permute-start.36 = (bf16[64,2048]{1,0:T(8,128)(2,1)S(1)}, bf16[64,2048]{1,0:T(8,128)(2,1)S(1)}, u32[]{:S(2)}, u32[]{:S(2)}) collective-permute-start(bf16[64,2048]{1,0:T(8,128)(2,1)S(1)} %get-tuple-element.368), channel_id=1, source_target_pairs={{2,0},{4,2},{6,4},{7,6},{5,7},{3,5},{1,3},{0,1},{10,8},{12,10},{14... | collective-permute-start | bytes 786440 | tf_op jit(solution)/shard_map/ppermute | solution.py:766
  289.8 18.0 %collective-permute-start.37 = (bf16[128,2048]{1,0:T(8,128)(2,1)S(1)}, bf16[128,2048]{1,0:T(8,128)(2,1)}, u32[]{:S(2)}, u32[]{:S(2)}) collective-permute-start(bf16[128,2048]{1,0:T(8,128)(2,1)S(1)} %get-tuple-element.379), channel_id=1, source_target_pairs={{0,2},{2,4},{4,6},{6,7},{7,5},{5,3},{3,1},{1,0},{8,10},{10,12},{12... | collective-permute-start | bytes 1572872 | tf_op jit(solution)/shard_map/ppermute | solution.py:763
  292.0 15.8 %collective-permute-start.38 = (bf16[128,2048]{1,0:T(8,128)(2,1)S(1)}, bf16[128,2048]{1,0:T(8,128)(2,1)}, u32[]{:S(2)}, u32[]{:S(2)}) collective-permute-start(bf16[128,2048]{1,0:T(8,128)(2,1)S(1)} %get-tuple-element.380), channel_id=1, source_target_pairs={{2,0},{4,2},{6,4},{7,6},{5,7},{3,5},{1,3},{0,1},{10,8},{12,10},{14... | collective-permute-start | bytes 1572872 | tf_op jit(solution)/shard_map/ppermute | solution.py:766
  292.0 15.8 %collective-permute-start.39 = (bf16[128,2048]{1,0:T(8,128)(2,1)S(1)}, bf16[128,2048]{1,0:T(8,128)(2,1)}, u32[]{:S(2)}, u32[]{:S(2)}) collective-permute-start(bf16[128,2048]{1,0:T(8,128)(2,1)S(1)} %get-tuple-element.381), channel_id=1, source_target_pairs={{0,2},{2,4},{4,6},{6,7},{7,5},{5,3},{3,1},{1,0},{8,10},{10,12},{12... | collective-permute-start | bytes 1572872 | tf_op jit(solution)/shard_map/ppermute | solution.py:763
  294.0 16.0 %collective-permute-start.40 = (bf16[128,2048]{1,0:T(8,128)(2,1)S(1)}, bf16[128,2048]{1,0:T(8,128)(2,1)}, u32[]{:S(2)}, u32[]{:S(2)}) collective-permute-start(bf16[128,2048]{1,0:T(8,128)(2,1)S(1)} %get-tuple-element.382), channel_id=1, source_target_pairs={{2,0},{4,2},{6,4},{7,6},{5,7},{3,5},{1,3},{0,1},{10,8},{12,10},{14... | collective-permute-start | bytes 1572872 | tf_op jit(solution)/shard_map/ppermute | solution.py:766
  315.7 12.3 %collective-permute-start.41 = (bf16[128,2048]{1,0:T(8,128)(2,1)}, bf16[128,2048]{1,0:T(8,128)(2,1)S(1)}, u32[]{:S(2)}, u32[]{:S(2)}) collective-permute-start(bf16[128,2048]{1,0:T(8,128)(2,1)} %get-tuple-element.398), channel_id=1, source_target_pairs={{0,2},{2,4},{4,6},{6,7},{7,5},{5,3},{3,1},{1,0},{8,10},{10,12},{12... | collective-permute-start | bytes 1572872 | tf_op jit(solution)/shard_map/ppermute | solution.py:763
  318.2 12.5 %collective-permute-start.42 = (bf16[128,2048]{1,0:T(8,128)(2,1)}, bf16[128,2048]{1,0:T(8,128)(2,1)S(1)}, u32[]{:S(2)}, u32[]{:S(2)}) collective-permute-start(bf16[128,2048]{1,0:T(8,128)(2,1)} %get-tuple-element.399), channel_id=1, source_target_pairs={{2,0},{4,2},{6,4},{7,6},{5,7},{3,5},{1,3},{0,1},{10,8},{12,10},{14... | collective-permute-start | bytes 1572872 | tf_op jit(solution)/shard_map/ppermute | solution.py:766
  318.2 21.0 %collective-permute-start.43 = (bf16[128,2048]{1,0:T(8,128)(2,1)}, bf16[128,2048]{1,0:T(8,128)(2,1)}, u32[]{:S(2)}, u32[]{:S(2)}) collective-permute-start(bf16[128,2048]{1,0:T(8,128)(2,1)} %get-tuple-element.400), channel_id=1, source_target_pairs={{0,2},{2,4},{4,6},{6,7},{7,5},{5,3},{3,1},{1,0},{8,10},{10,12},{12... | collective-permute-start | bytes 1572872 | tf_op jit(solution)/shard_map/ppermute | solution.py:763
  320.2 21.8 %collective-permute-start.44 = (bf16[128,2048]{1,0:T(8,128)(2,1)}, bf16[128,2048]{1,0:T(8,128)(2,1)}, u32[]{:S(2)}, u32[]{:S(2)}) collective-permute-start(bf16[128,2048]{1,0:T(8,128)(2,1)} %get-tuple-element.401), channel_id=1, source_target_pairs={{2,0},{4,2},{6,4},{7,6},{5,7},{3,5},{1,3},{0,1},{10,8},{12,10},{14... | collective-permute-start | bytes 1572872 | tf_op jit(solution)/shard_map/ppermute | solution.py:766
  344.0 12.7 %collective-permute-start.45 = (bf16[128,2048]{1,0:T(8,128)(2,1)S(1)}, bf16[128,2048]{1,0:T(8,128)(2,1)S(1)}, u32[]{:S(2)}, u32[]{:S(2)}) collective-permute-start(bf16[128,2048]{1,0:T(8,128)(2,1)S(1)} %get-tuple-element.406), channel_id=1, source_target_pairs={{0,2},{2,4},{4,6},{6,7},{7,5},{5,3},{3,1},{1,0},{8,10},{10,12},{12... | collective-permute-start | bytes 1572872 | tf_op jit(solution)/shard_map/ppermute | solution.py:763
  344.8 12.9 %collective-permute-start.46 = (bf16[128,2048]{1,0:T(8,128)(2,1)S(1)}, bf16[128,2048]{1,0:T(8,128)(2,1)S(1)}, u32[]{:S(2)}, u32[]{:S(2)}) collective-permute-start(bf16[128,2048]{1,0:T(8,128)(2,1)S(1)} %get-tuple-element.407), channel_id=1, source_target_pairs={{2,0},{4,2},{6,4},{7,6},{5,7},{3,5},{1,3},{0,1},{10,8},{12,10},{14... | collective-permute-start | bytes 1572872 | tf_op jit(solution)/shard_map/ppermute | solution.py:766
  346.1 18.4 %collective-permute-start.47 = (bf16[128,2048]{1,0:T(8,128)(2,1)S(1)}, bf16[128,2048]{1,0:T(8,128)(2,1)S(1)}, u32[]{:S(2)}, u32[]{:S(2)}) collective-permute-start(bf16[128,2048]{1,0:T(8,128)(2,1)S(1)} %get-tuple-element.408), channel_id=1, source_target_pairs={{0,2},{2,4},{4,6},{6,7},{7,5},{5,3},{3,1},{1,0},{8,10},{10,12},{12... | collective-permute-start | bytes 1572872 | tf_op jit(solution)/shard_map/ppermute | solution.py:763
  346.8 18.4 %collective-permute-start.48 = (bf16[128,2048]{1,0:T(8,128)(2,1)S(1)}, bf16[128,2048]{1,0:T(8,128)(2,1)S(1)}, u32[]{:S(2)}, u32[]{:S(2)}) collective-permute-start(bf16[128,2048]{1,0:T(8,128)(2,1)S(1)} %get-tuple-element.409), channel_id=1, source_target_pairs={{2,0},{4,2},{6,4},{7,6},{5,7},{3,5},{1,3},{0,1},{10,8},{12,10},{14... | collective-permute-start | bytes 1572872 | tf_op jit(solution)/shard_map/ppermute | solution.py:766
  367.7 12.3 %collective-permute-start.49 = (bf16[128,2048]{1,0:T(8,128)(2,1)S(1)}, bf16[128,2048]{1,0:T(8,128)(2,1)S(1)}, u32[]{:S(2)}, u32[]{:S(2)}) collective-permute-start(bf16[128,2048]{1,0:T(8,128)(2,1)S(1)} %get-tuple-element.446.refs_9_), channel_id=1, source_target_pairs={{0,2},{2,4},{4,6},{6,7},{7,5},{5,3},{3,1},{1,0},{8,10},{10,12},{12... | collective-permute-start | bytes 1572872 | tf_op jit(solution)/shard_map/ppermute | solution.py:763
  367.8 12.3 %collective-permute-start.50 = (bf16[128,2048]{1,0:T(8,128)(2,1)S(1)}, bf16[128,2048]{1,0:T(8,128)(2,1)S(1)}, u32[]{:S(2)}, u32[]{:S(2)}) collective-permute-start(bf16[128,2048]{1,0:T(8,128)(2,1)S(1)} %get-tuple-element.446.refs_9_), channel_id=1, source_target_pairs={{2,0},{4,2},{6,4},{7,6},{5,7},{3,5},{1,3},{0,1},{10,8},{12,10},{14... | collective-permute-start | bytes 1572872 | tf_op jit(solution)/shard_map/ppermute | solution.py:766
  369.9 13.4 %collective-permute-start.58 = (bf16[192,2048]{1,0:T(8,128)(2,1)S(1)}, bf16[192,2048]{1,0:T(8,128)(2,1)S(1)}, u32[]{:S(2)}, u32[]{:S(2)}) collective-permute-start(bf16[192,2048]{1,0:T(8,128)(2,1)S(1)} %get-tuple-element.500), channel_id=1, source_target_pairs={{0,8},{8,0},{16,24},{24,16},{1,9},{9,1},{17,25},{25,17},{2,10},{10... | collective-permute-start | bytes 2359304 | tf_op jit(solution)/shard_map/ppermute | solution.py:860
  370.0 39.3 %collective-permute-start.57 = (bf16[192,2048]{1,0:T(8,128)(2,1)S(1)}, bf16[192,2048]{1,0:T(8,128)(2,1)S(1)}, u32[]{:S(2)}, u32[]{:S(2)}) collective-permute-start(bf16[192,2048]{1,0:T(8,128)(2,1)S(1)} %get-tuple-element.499), channel_id=1, source_target_pairs={{0,8},{8,0},{16,24},{24,16},{1,9},{9,1},{17,25},{25,17},{2,10},{10... | collective-permute-start | bytes 2359304 | tf_op jit(solution)/shard_map/ppermute | solution.py:860
  380.1 13.6 %collective-permute-start.51 = (bf16[128,2048]{1,0:T(8,128)(2,1)S(1)}, bf16[128,2048]{1,0:T(8,128)(2,1)S(1)}, u32[]{:S(2)}, u32[]{:S(2)}) collective-permute-start(bf16[128,2048]{1,0:T(8,128)(2,1)S(1)} %collective-permute-done.49.refs_10_), channel_id=1, source_target_pairs={{0,2},{2,4},{4,6},{6,7},{7,5},{5,3},{3,1},{1,0},{8,10},{10,12},{12... | collective-permute-start | bytes 1572872 | tf_op jit(solution)/shard_map/ppermute | solution.py:763
  380.1 13.6 %collective-permute-start.52 = (bf16[128,2048]{1,0:T(8,128)(2,1)S(1)}, bf16[128,2048]{1,0:T(8,128)(2,1)S(1)}, u32[]{:S(2)}, u32[]{:S(2)}) collective-permute-start(bf16[128,2048]{1,0:T(8,128)(2,1)S(1)} %collective-permute-done.50.refs_11_), channel_id=1, source_target_pairs={{2,0},{4,2},{6,4},{7,6},{5,7},{3,5},{1,3},{0,1},{10,8},{12,10},{14... | collective-permute-start | bytes 1572872 | tf_op jit(solution)/shard_map/ppermute | solution.py:766
  383.6 25.7 %collective-permute-start.59 = (bf16[192,2048]{1,0:T(8,128)(2,1)S(1)}, bf16[192,2048]{1,0:T(8,128)(2,1)S(1)}, u32[]{:S(2)}, u32[]{:S(2)}) collective-permute-start(bf16[192,2048]{1,0:T(8,128)(2,1)S(1)} %add_convert_fusion), channel_id=1, source_target_pairs={{0,16},{8,24},{16,0},{24,8},{1,17},{9,25},{17,1},{25,9},{2,18},{10... | collective-permute-start | bytes 2359304 | tf_op jit(solution)/shard_map/ppermute | solution.py:860
  393.7 12.4 %collective-permute-start.53 = (bf16[128,2048]{1,0:T(8,128)(2,1)S(1)}, bf16[128,2048]{1,0:T(8,128)(2,1)S(1)}, u32[]{:S(2)}, u32[]{:S(2)}) collective-permute-start(bf16[128,2048]{1,0:T(8,128)(2,1)S(1)} %collective-permute-done.51.refs_12_), channel_id=1, source_target_pairs={{0,2},{2,4},{4,6},{6,7},{7,5},{5,3},{3,1},{1,0},{8,10},{10,12},{12... | collective-permute-start | bytes 1572872 | tf_op jit(solution)/shard_map/ppermute | solution.py:763
  393.7 12.3 %collective-permute-start.54 = (bf16[128,2048]{1,0:T(8,128)(2,1)S(1)}, bf16[128,2048]{1,0:T(8,128)(2,1)S(1)}, u32[]{:S(2)}, u32[]{:S(2)}) collective-permute-start(bf16[128,2048]{1,0:T(8,128)(2,1)S(1)} %collective-permute-done.52.refs_13_), channel_id=1, source_target_pairs={{2,0},{4,2},{6,4},{7,6},{5,7},{3,5},{1,3},{0,1},{10,8},{12,10},{14... | collective-permute-start | bytes 1572872 | tf_op jit(solution)/shard_map/ppermute | solution.py:766
  423.4 36.8 %all-to-all-start.2 = ((bf16[8,64,1536]{2,1,0:T(8,128)(2,1)}), bf16[8,64,1536]{2,1,0:T(8,128)(2,1)}, u32[]{:S(2)}, u32[]{:S(2)}) async-start(bf16[8,64,1536]{2,1,0:T(8,128)(2,1)} %bitcast.77), calls=%async_computation.3 | async-start | bytes 3145728 | tf_op jit(solution)/shard_map/all_to_all | solution.py:876
  430.2 58.5 %reduce-scatter.5.cloned.1.call-start = ((), (), s32[]{:S(2)}) async-start(), calls=%async_computation.11 | async-start | bytes 1310720 | tf_op jit(solution)/shard_map/reduce_scatter | solution.py:857
  442.4 17.9 %collective-permute-start.60 = (bf16[64,2048]{1,0:T(8,128)(2,1)}, bf16[64,2048]{1,0:T(8,128)(2,1)}, u32[]{:S(2)}, u32[]{:S(2)}) collective-permute-start(bf16[64,2048]{1,0:T(8,128)(2,1)} %get-tuple-element.441), channel_id=1, source_target_pairs={{0,2},{2,4},{4,6},{6,7},{7,5},{5,3},{3,1},{1,0},{8,10},{10,12},{12... | collective-permute-start | bytes 786440 | tf_op jit(solution)/shard_map/ppermute | solution.py:763
  444.4 15.9 %collective-permute-start.61 = (bf16[64,2048]{1,0:T(8,128)(2,1)}, bf16[64,2048]{1,0:T(8,128)(2,1)}, u32[]{:S(2)}, u32[]{:S(2)}) collective-permute-start(bf16[64,2048]{1,0:T(8,128)(2,1)} %get-tuple-element.442), channel_id=1, source_target_pairs={{2,0},{4,2},{6,4},{7,6},{5,7},{3,5},{1,3},{0,1},{10,8},{12,10},{14... | collective-permute-start | bytes 786440 | tf_op jit(solution)/shard_map/ppermute | solution.py:766
  444.5 21.6 %collective-permute-start.68 = (bf16[640,512]{1,0:T(8,128)(2,1)}, bf16[640,512]{1,0:T(8,128)(2,1)S(1)}, u32[]{:S(2)}, u32[]{:S(2)}) collective-permute-start(bf16[640,512]{1,0:T(8,128)(2,1)} %get-tuple-element.501), channel_id=1, source_target_pairs={{0,8},{8,0},{16,24},{24,16},{1,9},{9,1},{17,25},{25,17},{2,10},{10... | collective-permute-start | bytes 1966088 | tf_op jit(solution)/shard_map/ppermute | solution.py:860
  451.8 20.4 %collective-permute-start.70 = (bf16[640,512]{1,0:T(8,128)(2,1)S(1)}, bf16[640,512]{1,0:T(8,128)(2,1)S(1)}, u32[]{:S(2)}, u32[]{:S(2)}) collective-permute-start(bf16[640,512]{1,0:T(8,128)(2,1)S(1)} %add_convert_fusion.2), channel_id=1, source_target_pairs={{0,16},{8,24},{16,0},{24,8},{1,17},{9,25},{17,1},{25,9},{2,18},{10... | collective-permute-start | bytes 1966088 | tf_op jit(solution)/shard_map/ppermute | solution.py:860
  462.6 21.1 %collective-permute-start.62 = (bf16[128,2048]{1,0:T(8,128)(2,1)}, bf16[128,2048]{1,0:T(8,128)(2,1)}, u32[]{:S(2)}, u32[]{:S(2)}) collective-permute-start(bf16[128,2048]{1,0:T(8,128)(2,1)} %get-tuple-element.460), channel_id=1, source_target_pairs={{0,2},{2,4},{4,6},{6,7},{7,5},{5,3},{3,1},{1,0},{8,10},{10,12},{12... | collective-permute-start | bytes 1572872 | tf_op jit(solution)/shard_map/ppermute | solution.py:763
  466.1 17.6 %collective-permute-start.63 = (bf16[128,2048]{1,0:T(8,128)(2,1)S(1)}, bf16[128,2048]{1,0:T(8,128)(2,1)}, u32[]{:S(2)}, u32[]{:S(2)}) collective-permute-start(bf16[128,2048]{1,0:T(8,128)(2,1)S(1)} %get-tuple-element.461), channel_id=1, source_target_pairs={{2,0},{4,2},{6,4},{7,6},{5,7},{3,5},{1,3},{0,1},{10,8},{12,10},{14... | collective-permute-start | bytes 1572872 | tf_op jit(solution)/shard_map/ppermute | solution.py:766
  474.4 39.5 %all-to-all-start.3 = ((bf16[8,80,512]{2,1,0:T(8,128)(2,1)}), bf16[8,80,512]{2,1,0:T(8,128)(2,1)S(1)}, u32[]{:S(2)}, u32[]{:S(2)}) async-start(bf16[8,80,512]{2,1,0:T(8,128)(2,1)} %bitcast.13), calls=%async_computation.4 | async-start | bytes 1310720 | tf_op jit(solution)/shard_map/all_to_all | solution.py:876
  486.6 16.1 %collective-permute-start.64 = (bf16[128,2048]{1,0:T(8,128)(2,1)}, bf16[128,2048]{1,0:T(8,128)(2,1)S(1)}, u32[]{:S(2)}, u32[]{:S(2)}) collective-permute-start(bf16[128,2048]{1,0:T(8,128)(2,1)} %get-tuple-element.467), channel_id=1, source_target_pairs={{0,2},{2,4},{4,6},{6,7},{7,5},{5,3},{3,1},{1,0},{8,10},{10,12},{12... | collective-permute-start | bytes 1572872 | tf_op jit(solution)/shard_map/ppermute | solution.py:763
  488.6 17.7 %collective-permute-start.65 = (bf16[128,2048]{1,0:T(8,128)(2,1)S(1)}, bf16[128,2048]{1,0:T(8,128)(2,1)}, u32[]{:S(2)}, u32[]{:S(2)}) collective-permute-start(bf16[128,2048]{1,0:T(8,128)(2,1)S(1)} %get-tuple-element.468), channel_id=1, source_target_pairs={{2,0},{4,2},{6,4},{7,6},{5,7},{3,5},{1,3},{0,1},{10,8},{12,10},{14... | collective-permute-start | bytes 1572872 | tf_op jit(solution)/shard_map/ppermute | solution.py:766
  488.6 24.5 %collective-permute-start.71 = (bf16[64,2048]{1,0:T(8,128)(2,1)}, bf16[64,2048]{1,0:T(8,128)(2,1)S(1)}, u32[]{:S(2)}, u32[]{:S(2)}) collective-permute-start(bf16[64,2048]{1,0:T(8,128)(2,1)} %reduce-scatter.5.cloned.1.call-done), channel_id=1, source_target_pairs={{0,0},{8,1},{16,2},{24,3},{4,4},{12,5},{20,6},{28,7},{1,8},{9,9},{... | collective-permute-start | bytes 786440 | tf_op jit(solution)/shard_map/ppermute | solution.py:885
  509.2 13.8 %collective-permute-start.66 = (bf16[128,2048]{1,0:T(8,128)(2,1)}, bf16[128,2048]{1,0:T(8,128)(2,1)S(1)}, u32[]{:S(2)}, u32[]{:S(2)}) collective-permute-start(bf16[128,2048]{1,0:T(8,128)(2,1)} %get-tuple-element.471), channel_id=1, source_target_pairs={{0,2},{2,4},{4,6},{6,7},{7,5},{5,3},{3,1},{1,0},{8,10},{10,12},{12... | collective-permute-start | bytes 1572872 | tf_op jit(solution)/shard_map/ppermute | solution.py:763
  512.5 12.6 %collective-permute-start.67 = (bf16[128,2048]{1,0:T(8,128)(2,1)}, bf16[128,2048]{1,0:T(8,128)(2,1)S(1)}, u32[]{:S(2)}, u32[]{:S(2)}) collective-permute-start(bf16[128,2048]{1,0:T(8,128)(2,1)} %get-tuple-element.472), channel_id=1, source_target_pairs={{2,0},{4,2},{6,4},{7,6},{5,7},{3,5},{1,3},{0,1},{10,8},{12,10},{14... | collective-permute-start | bytes 1572872 | tf_op jit(solution)/shard_map/ppermute | solution.py:766
  (98 other events, 1098.3 us)
Sparse Core Ops, SparseCore 0:
  52.6 28.1 all-gather.4
  82.4 28.5 all-gather.6
  125.6 21.9 all-gather.8
  171.1 43.5 all-gather.10
  310.2 60.1 reduce-scatter.2
  450.4 29.7 reduce-scatter.4

commit v2 on v1

--- a/solution.py
+++ b/solution.py
@@ -978,12 +978,12 @@
     def sum_gu(sent):
         return {
             "gu": outer_sum(
-                hold(pieces_two, sent), [singly(grad_gate_act), singly(grad_up_act)], 256
+                hold(pieces_two, sent), [singly(grad_gate_act), singly(grad_up_act)], 512
             )
         }
 
     def sum_down(sent):
-        done["down"] = outer_sum(singly(hold(hidden, sent)), [pieces_c], 256)
+        done["down"] = outer_sum(singly(hold(hidden, sent)), [pieces_c], 384)
         return done["down"]
 
     grad_normed_two, summed = ring_scatter([part_two, part_out], [sum_down, sum_gu])

time: 546 us -> 546 us (level)
  transfers between devices with their start and end apart: 82 -> 82, of which waited for: 51 -> 52; matrix products, arithmetic and copies ran while one was open for 12% -> 12% of each run, Pallas kernels for 14% -> 14%
where the time goes in v2:
time: 546 us; the launch traced here: 536 us
  waiting for transfers between devices  225 us (41%)
  starting transfers between devices  115 us (21%)
  Pallas kernels  77.4 us (14%)
  local copies, waits for them, and re-layouts  50 us (9%)
  other arithmetic  41.3 us (8%)
  between operations  15.8 us (3%)
  matrix products  12.5 us (2%)
    ppermute x32, waiting for transfers between devices, right(): return lax.ppermute(value, 'ctx', onward)  171 us
    ppermute x32, starting transfers between devices, right(): return lax.ppermute(value, 'ctx', onward)  54.3 us
    ppermute x32, waiting for transfers between devices, left(): return lax.ppermute(value, 'ctx', backward)  43 us
    unnamed x162, local copies, waits for them, and re-layouts  32.9 us
    pallas_call x5, Pallas kernels, feed(): pl.pallas_call(partial(feed_kernel, count), out_shape=[jax.ShapeDtypeStru...  28 us
    ppermute x32, starting transfers between devices, left(): return lax.ppermute(value, 'ctx', backward)  26.7 us
    all_to_all x4, starting transfers between devices, turn(): return lax.all_to_all(value, 'ctx', split_axis=0, concat_axis=0, tiled=True)  21.5 us
    pallas_call x3, Pallas kernels, outer_sum(): pl.pallas_call(partial(outer_kernel, [len(group) for group in lefts], [[l...  18.4 us
  transfers between devices with their start and end apart: 82, of which 52 were waited for; matrix products, arithmetic and copies ran while one was open for 12% of the time, Pallas kernels for 14%

profile of v2, /device:TPU:0, one launch (start us, length us, event | category | flops | bytes accessed | tf_op | source)
XLA Modules:
  0.0 536.0 jit_solution(5588436102510898875)
XLA Ops:
  7.2 3.1 collective-permute-start
  13.6 8.7 %collective-permute-done = bf16[128,2048]{1,0:T(8,128)(2,1)S(1)} collective-permute-done((bf16[128,2048]{1,0:T(8,128)(2,1)}, bf16[128,2048]{1,0:T(8,128)(2,1)S(1)}, u32[]{:S(2)}, u32[]{:S(2)}) %collective-permute-start) | collective-permute-done | bytes 524320 | tf_op jit(solution)/shard_map/ppermute | solution.py:763
  23.9 4.8 all-to-all-start
  30.8 2.8 shard_map.238
  33.6 15.9 %collective-permute-done.2 = bf16[128,2048]{1,0:T(8,128)(2,1)S(1)} collective-permute-done((bf16[128,2048]{1,0:T(8,128)(2,1)S(1)}, bf16[128,2048]{1,0:T(8,128)(2,1)S(1)}, u32[]{:S(2)}, u32[]{:S(2)}) %collective-permute-start.2) | collective-permute-done | bytes 524320 | tf_op jit(solution)/shard_map/ppermute | solution.py:763
  53.3 2.5 broadcast_in_dim.32
  57.5 5.0 collective-permute-start.4
  65.0 7.0 %collective-permute-done.4 = bf16[128,2048]{1,0:T(8,128)(2,1)S(1)} collective-permute-done((bf16[128,2048]{1,0:T(8,128)(2,1)S(1)}, bf16[128,2048]{1,0:T(8,128)(2,1)S(1)}, u32[]{:S(2)}, u32[]{:S(2)}) %collective-permute-start.4) | collective-permute-done | bytes 524320 | tf_op jit(solution)/shard_map/ppermute | solution.py:763
  81.8 4.3 all-to-all-start.1
  94.8 6.2 %shard_map.239 = (bf16[1024,2048]{1,0:T(8,128)(2,1)S(1)}, f32[1024,384]{1,0:T(8,128)S(1)}, bf16[1024,256]{1,0:T(8,128)(2,1)S(1)}, bf16[1024,128]{1,0:T(8,128)(2,...) custom-call(bf16[1024,2048]{1,0:T(8,128)(2,1)} %constant_dynamic-update-slice_fusion.7.tokens, ...), custom_call_target="tpu_custom_call" | custom-call | flops 2147483648 | bytes 14000000 | tf_op jit(solution)/shard_map/pallas_call | solution.py:435
  107.1 13.7 %collective-permute-done.8.refs_2_.refs_6_ = bf16[128,2048]{1,0:T(8,128)(2,1)S(1)} collective-permute-done((bf16[128,2048]{1,0:T(8,128)(2,1)S(1)}, bf16[128,2048]{1,0:T(8,128)(2,1)S(1)}, u32[]{:S(2)}, u32[]{:S(2)}) %collective-permute-start.8) | collective-permute-done | bytes 524320 | tf_op jit(solution)/shard_map/ppermute | solution.py:763
  120.8 4.7 collective-permute-done.9.refs_3_.refs_7_
  125.5 7.4 %collective-permute-start.11 = (bf16[128,2048]{1,0:T(8,128)(2,1)S(1)}, bf16[128,2048]{1,0:T(8,128)(2,1)S(1)}, u32[]{:S(2)}, u32[]{:S(2)}) collective-permute-start(bf16[128,2048]{1,0:T(8,128)(2,1)S(1)} %collective-permute-done.8.refs_2_.refs_6_), channel_id=1, source_target_pairs={{0,2},{2,4},{4,6},{6,7},{7,5},{5,3},{3,1},{1,0},{8,10},{10,12},{12... | collective-permute-start | bytes 1572872 | tf_op jit(solution)/shard_map/ppermute | solution.py:763
  135.1 4.5 shard_map.240
  140.4 4.3 collective-permute-done.11.refs_2_.refs_8_
  149.8 10.3 %collective-permute-done.13.refs_2_.refs_10_ = bf16[128,2048]{1,0:T(8,128)(2,1)S(1)} collective-permute-done((bf16[128,2048]{1,0:T(8,128)(2,1)S(1)}, bf16[128,2048]{1,0:T(8,128)(2,1)S(1)}, u32[]{:S(2)}, u32[]{:S(2)}) %collective-permute-start.13) | collective-permute-done | bytes 524320 | tf_op jit(solution)/shard_map/ppermute | solution.py:763
  164.8 4.8 collective-permute-done.15.refs_2_.refs_12_
  176.0 4.5 collective-permute-done.17
  184.0 8.3 %collective-permute-done.19 = bf16[128,2048]{1,0:T(8,128)(2,1)S(1)} collective-permute-done((bf16[128,2048]{1,0:T(8,128)(2,1)S(1)}, bf16[128,2048]{1,0:T(8,128)(2,1)S(1)}, u32[]{:S(2)}, u32[]{:S(2)}) %collective-permute-start.19) | collective-permute-done | bytes 524320 | tf_op jit(solution)/shard_map/ppermute | solution.py:763
  196.0 7.8 %collective-permute-done.21 = bf16[128,2048]{1,0:T(8,128)(2,1)S(1)} collective-permute-done((bf16[128,2048]{1,0:T(8,128)(2,1)S(1)}, bf16[128,2048]{1,0:T(8,128)(2,1)S(1)}, u32[]{:S(2)}, u32[]{:S(2)}) %collective-permute-start.21) | collective-permute-done | bytes 524320 | tf_op jit(solution)/shard_map/ppermute | solution.py:763
  208.2 7.4 %collective-permute-done.23 = bf16[128,2048]{1,0:T(8,128)(2,1)} collective-permute-done((bf16[128,2048]{1,0:T(8,128)(2,1)}, bf16[128,2048]{1,0:T(8,128)(2,1)}, u32[]{:S(2)}, u32[]{:S(2)}) %collective-permute-start.23) | collective-permute-done | bytes 524320 | tf_op jit(solution)/shard_map/ppermute | solution.py:763
  221.9 2.8 copy-done
  225.7 5.6 %shard_map.241 = (bf16[128,768]{1,0:T(8,128)(2,1)S(1)}, bf16[128,768]{1,0:T(8,128)(2,1)S(1)}, bf16[128,768]{1,0:T(8,128)(2,1)S(1)}, bf16[128,2048]{1,0:T(8,128)(2,1)S(1)}, bf16[128,2048]{1,0:T(8,128)(2,1)S(1)}) custom-call(bf16[128,2048]{1,0:T(8,128)(2,1)} %multiply_convert_fusion.refs_0_, bf16[128,2048]{1,0:T(8,128)(2,1)S(1)} %bitcast.68, ...), custom_call_target="tpu_custom_call" | custom-call | flops 2415919104 | bytes 12582912 | tf_op jit(solution)/shard_map/pallas_call | solution.py:661
  235.0 6.4 %shard_map.242 = (bf16[256,768]{1,0:T(8,128)(2,1)S(1)}, bf16[256,768]{1,0:T(8,128)(2,1)S(1)}, bf16[256,768]{1,0:T(8,128)(2,1)S(1)}, bf16[256,2048]{1,0:T(8,128)(2,1)S(1)}, bf16[256,2048]{1,0:T(8,128)(2,1)S(1)}) custom-call(bf16[128,2048]{1,0:T(8,128)(2,1)} %collective-permute-done.25.refs_0_.refs_1_, ...), custom_call_target="tpu_custom_call" | custom-call | flops 4831838208 | bytes 15728640 | tf_op jit(solution)/shard_map/pallas_call | solution.py:661
  243.4 2.7 collective-permute-done.27.refs_0_.refs_3_
  248.6 6.3 %shard_map.243 = (bf16[256,768]{1,0:T(8,128)(2,1)S(1)}, bf16[256,768]{1,0:T(8,128)(2,1)S(1)}, bf16[256,768]{1,0:T(8,128)(2,1)S(1)}, bf16[256,2048]{1,0:T(8,128)(2,1)S(1)}, bf16[256,2048]{1,0:T(8,128)(2,1)S(1)}) custom-call(bf16[128,2048]{1,0:T(8,128)(2,1)S(1)} %collective-permute-done.27.refs_0_.refs_3_, ...), custom_call_target="tpu_custom_call" | custom-call | flops 4831838208 | bytes 15728640 | tf_op jit(solution)/shard_map/pallas_call | solution.py:661
  260.8 5.2 shard_map.244
  267.0 4.4 shard_map.245
  273.9 2.9 collective-permute-start.35
  276.9 5.6 %shard_map.246 = bf16[768,2048]{1,0:T(8,128)(2,1)S(1)} custom-call(bf16[128,768]{1,0:T(8,128)(2,1)S(1)} %get-tuple-element.370.refs_0_, bf16[256,768]{1,0:T(8,128)(2,1)S(1)} %get-tuple-element.371.refs_1_, bf16[256,768]{1,0:T(8,128)(2,1)S(1)} %get-tuple-element.372.refs_2_, bf16[256,768]{1,0:T(8,128)(2,1)S(1)} %get-tuple-element.373.refs_3_, ...), custom_call_target="tpu_custom_call" | custom-call | flops 3221225472 | bytes 8912896 | tf_op jit(solution)/shard_map/pallas_call | solution.py:699
  283.8 2.5 collective-permute-done.35
  286.4 3.1 collective-permute-done.36
  294.0 10.2 %shard_map.247 = bf16[2048,1536]{1,0:T(8,128)(2,1)S(1)} custom-call(bf16[128,2048]{1,0:T(8,128)(2,1)} %multiply_convert_fusion.refs_0_, bf16[128,2048]{1,0:T(8,128)(2,1)} %collective-permute-done.25.refs_0_.refs_1_, bf16[128,2048]{1,0:T(8,128)(2,1)} %collective-permute-done.26.refs_1_.refs_2_, bf16[128,2048]{1,0:T(8,128)(2,1)S(1)} %collective-permute-done.27.refs_0_.refs_3_, ...), custom_call_target="tpu_custom_call" | custom-call | flops 6442450944 | bytes 13631488 | tf_op jit(solution)/shard_map/pallas_call | solution.py:699
  304.3 2.7 copy-done.2
  307.2 2.9 collective-permute-done.40
  310.1 3.0 add_convert_fusion.14
  313.1 2.6 add_convert_fusion.16
  320.2 7.8 %collective-permute-done.41 = bf16[128,2048]{1,0:T(8,128)(2,1)S(1)} collective-permute-done((bf16[128,2048]{1,0:T(8,128)(2,1)}, bf16[128,2048]{1,0:T(8,128)(2,1)S(1)}, u32[]{:S(2)}, u32[]{:S(2)}) %collective-permute-start.41) | collective-permute-done | bytes 524320 | tf_op jit(solution)/shard_map/ppermute | solution.py:763
  328.0 2.7 collective-permute-done.42
  330.6 8.6 %collective-permute-done.43 = bf16[128,2048]{1,0:T(8,128)(2,1)} collective-permute-done((bf16[128,2048]{1,0:T(8,128)(2,1)}, bf16[128,2048]{1,0:T(8,128)(2,1)}, u32[]{:S(2)}, u32[]{:S(2)}) %collective-permute-start.43) | collective-permute-done | bytes 524320 | tf_op jit(solution)/shard_map/ppermute | solution.py:763
  339.2 2.8 collective-permute-done.44
  348.1 3.1 fusion
  351.2 5.5 %collective-permute-done.45 = bf16[128,2048]{1,0:T(8,128)(2,1)S(1)} collective-permute-done((bf16[128,2048]{1,0:T(8,128)(2,1)S(1)}, bf16[128,2048]{1,0:T(8,128)(2,1)S(1)}, u32[]{:S(2)}, u32[]{:S(2)}) %collective-permute-start.45) | collective-permute-done | bytes 524320 | tf_op jit(solution)/shard_map/ppermute | solution.py:763
  357.7 6.8 %collective-permute-done.47 = bf16[128,2048]{1,0:T(8,128)(2,1)S(1)} collective-permute-done((bf16[128,2048]{1,0:T(8,128)(2,1)S(1)}, bf16[128,2048]{1,0:T(8,128)(2,1)S(1)}, u32[]{:S(2)}, u32[]{:S(2)}) %collective-permute-start.47) | collective-permute-done | bytes 524320 | tf_op jit(solution)/shard_map/ppermute | solution.py:763
  371.0 9.0 %collective-permute-done.49.refs_10_ = bf16[128,2048]{1,0:T(8,128)(2,1)S(1)} collective-permute-done((bf16[128,2048]{1,0:T(8,128)(2,1)S(1)}, bf16[128,2048]{1,0:T(8,128)(2,1)S(1)}, u32[]{:S(2)}, u32[]{:S(2)}) %collective-permute-start.49) | collective-permute-done | bytes 524320 | tf_op jit(solution)/shard_map/ppermute | solution.py:763
  385.7 7.9 %collective-permute-done.51.refs_12_ = bf16[128,2048]{1,0:T(8,128)(2,1)S(1)} collective-permute-done((bf16[128,2048]{1,0:T(8,128)(2,1)S(1)}, bf16[128,2048]{1,0:T(8,128)(2,1)S(1)}, u32[]{:S(2)}, u32[]{:S(2)}) %collective-permute-start.51) | collective-permute-done | bytes 524320 | tf_op jit(solution)/shard_map/ppermute | solution.py:763
  393.7 2.6 collective-permute-start.54
  397.3 8.7 %collective-permute-done.53.refs_14_ = bf16[128,2048]{1,0:T(8,128)(2,1)S(1)} collective-permute-done((bf16[128,2048]{1,0:T(8,128)(2,1)S(1)}, bf16[128,2048]{1,0:T(8,128)(2,1)S(1)}, u32[]{:S(2)}, u32[]{:S(2)}) %collective-permute-start.53) | collective-permute-done | bytes 524320 | tf_op jit(solution)/shard_map/ppermute | solution.py:763
  414.6 7.6 %shard_map.248 = (bf16[1024,512]{1,0:T(8,128)(2,1)S(1)}, f32[1,128]{1,0:T(1,128)S(1)}, f32[1,128]{1,0:T(1,128)S(1)}) custom-call(bf16[1024,256]{1,0:T(8,128)(2,1)S(1)} %copy-done.57, bf16[1024,128]{1,0:T(8,128)(2,1)S(1)} %copy-done.59, bf16[1024,128]{1,0:T(8,128)(2,1)S(1)} %copy-done.62, s32[1024,1]{1,0:T(8,128)S(1)} %copy-done.34, ...), custom_call_target="tpu_custom_call" | custom-call | flops 2684354560 | bytes 6000000 | tf_op jit(solution)/shard_map/pallas_call | solution.py:576
  423.2 6.6 %all-to-all-start.2 = ((bf16[8,64,1536]{2,1,0:T(8,128)(2,1)}), bf16[8,64,1536]{2,1,0:T(8,128)(2,1)}, u32[]{:S(2)}, u32[]{:S(2)}) async-start(bf16[8,64,1536]{2,1,0:T(8,128)(2,1)} %bitcast.77), calls=%async_computation.3 | async-start | bytes 3145728 | tf_op jit(solution)/shard_map/all_to_all | solution.py:876
  430.1 5.7 %fusion.2 = (f32[2048]{0:T(1024)S(1)}, bf16[1024,2048]{1,0:T(8,128)(2,1)S(1)}) fusion(bf16[1024,2048]{1,0:T(8,128)(2,1)} %constant_dynamic-update-slice_fusion.7.tokens, f32[1024]{0:T(1024)S(1)} %add_rsqrt_fusion, bf16[1024,512]{1,0:T(8,128)(2,1)} %copy-done.53, bf16[2048,512]{1,0:T(8,128)(2,1)} %copy-done.50), kind=kOutput, calls=%fused_computation.4 | convolution fusion | flops 2157967360 | bytes 11546624 | tf_op jit(solution)/shard_map/dot_general | solution.py:56
  447.4 2.5 shard_map.250
  451.4 5.2 collective-permute-start.70
  456.6 3.3 all-to-all-done.2.turned
  462.3 3.5 collective-permute-start.62
  465.8 6.1 %collective-permute-done.70 = bf16[640,512]{1,0:T(8,128)(2,1)S(1)} collective-permute-done((bf16[640,512]{1,0:T(8,128)(2,1)S(1)}, bf16[640,512]{1,0:T(8,128)(2,1)S(1)}, u32[]{:S(2)}, u32[]{:S(2)}) %collective-permute-start.70) | collective-permute-done | bytes 655392 | tf_op jit(solution)/shard_map/ppermute | solution.py:860
  474.0 5.9 %all-to-all-start.3 = ((bf16[8,80,512]{2,1,0:T(8,128)(2,1)}), bf16[8,80,512]{2,1,0:T(8,128)(2,1)S(1)}, u32[]{:S(2)}, u32[]{:S(2)}) async-start(bf16[8,80,512]{2,1,0:T(8,128)(2,1)} %bitcast.13), calls=%async_computation.4 | async-start | bytes 1310720 | tf_op jit(solution)/shard_map/all_to_all | solution.py:876
  479.9 3.5 shard_map.251
  483.4 2.8 add_convert_fusion.5
  489.9 12.5 %collective-permute-done.64 = bf16[128,2048]{1,0:T(8,128)(2,1)S(1)} collective-permute-done((bf16[128,2048]{1,0:T(8,128)(2,1)}, bf16[128,2048]{1,0:T(8,128)(2,1)S(1)}, u32[]{:S(2)}, u32[]{:S(2)}) %collective-permute-start.64) | collective-permute-done | bytes 524320 | tf_op jit(solution)/shard_map/ppermute | solution.py:763
  502.3 3.7 collective-permute-done.65
  506.0 2.8 add_convert_fusion.3
  508.8 3.3 collective-permute-start.66
  519.1 3.5 collective-permute-done.66
  (372 shorter events, 169.8 us)
Async XLA Ops:
  7.2 15.1 %collective-permute-start = (bf16[128,2048]{1,0:T(8,128)(2,1)}, bf16[128,2048]{1,0:T(8,128)(2,1)S(1)}, u32[]{:S(2)}, u32[]{:S(2)}) collective-permute-start(bf16[128,2048]{1,0:T(8,128)(2,1)} %bitcast.74), channel_id=1, source_target_pairs={{0,2},{2,4},{4,6},{6,7},{7,5},{5,3},{3,1},{1,0},{8,10},{10,12},{12... | collective-permute-start | bytes 1572872 | tf_op jit(solution)/shard_map/ppermute | solution.py:763
  10.3 13.6 %collective-permute-start.1 = (bf16[128,2048]{1,0:T(8,128)(2,1)}, bf16[128,2048]{1,0:T(8,128)(2,1)S(1)}, u32[]{:S(2)}, u32[]{:S(2)}) collective-permute-start(bf16[128,2048]{1,0:T(8,128)(2,1)} %bitcast.75), channel_id=1, source_target_pairs={{2,0},{4,2},{6,4},{7,6},{5,7},{3,5},{1,3},{0,1},{10,8},{12,10},{14... | collective-permute-start | bytes 1572872 | tf_op jit(solution)/shard_map/ppermute | solution.py:766
  23.9 27.8 %all-to-all-start = ((bf16[8,80,512]{2,1,0:T(8,128)(2,1)}), bf16[8,80,512]{2,1,0:T(8,128)(2,1)S(1)}, u32[]{:S(2)}, u32[]{:S(2)}) async-start(bf16[8,80,512]{2,1,0:T(8,128)(2,1)} %shard_map.237), calls=%async_computation | async-start | bytes 1310720 | tf_op jit(solution)/shard_map/all_to_all | solution.py:876
  28.6 62.7 %all-gather.5.cloned.1.call-start = ((), (), s32[]{:S(2)}) async-start(), calls=%async_computation.6 | async-start | bytes 3276800 | tf_op jit(solution)/shard_map/all_gather | solution.py:854
  28.7 20.8 %collective-permute-start.2 = (bf16[128,2048]{1,0:T(8,128)(2,1)S(1)}, bf16[128,2048]{1,0:T(8,128)(2,1)S(1)}, u32[]{:S(2)}, u32[]{:S(2)}) collective-permute-start(bf16[128,2048]{1,0:T(8,128)(2,1)S(1)} %collective-permute-done), channel_id=1, source_target_pairs={{0,2},{2,4},{4,6},{6,7},{7,5},{5,3},{3,1},{1,0},{8,10},{10,12},{12... | collective-permute-start | bytes 1572872 | tf_op jit(solution)/shard_map/ppermute | solution.py:763
  30.7 20.9 %collective-permute-start.3 = (bf16[128,2048]{1,0:T(8,128)(2,1)S(1)}, bf16[128,2048]{1,0:T(8,128)(2,1)S(1)}, u32[]{:S(2)}, u32[]{:S(2)}) collective-permute-start(bf16[128,2048]{1,0:T(8,128)(2,1)S(1)} %collective-permute-done.1), channel_id=1, source_target_pairs={{2,0},{4,2},{6,4},{7,6},{5,7},{3,5},{1,3},{0,1},{10,8},{12,10},{14... | collective-permute-start | bytes 1572872 | tf_op jit(solution)/shard_map/ppermute | solution.py:766
  52.5 118.5 %all-gather.7.cloned.1.call-start = ((), (), s32[]{:S(2)}) async-start(), calls=%async_computation.7 | async-start | bytes 3932160 | tf_op jit(solution)/shard_map/all_gather | solution.py:854
  57.5 14.5 %collective-permute-start.4 = (bf16[128,2048]{1,0:T(8,128)(2,1)S(1)}, bf16[128,2048]{1,0:T(8,128)(2,1)S(1)}, u32[]{:S(2)}, u32[]{:S(2)}) collective-permute-start(bf16[128,2048]{1,0:T(8,128)(2,1)S(1)} %collective-permute-done.2), channel_id=1, source_target_pairs={{0,2},{2,4},{4,6},{6,7},{7,5},{5,3},{3,1},{1,0},{8,10},{10,12},{12... | collective-permute-start | bytes 1572872 | tf_op jit(solution)/shard_map/ppermute | solution.py:763
  62.5 11.7 %collective-permute-start.5 = (bf16[128,2048]{1,0:T(8,128)(2,1)S(1)}, bf16[128,2048]{1,0:T(8,128)(2,1)S(1)}, u32[]{:S(2)}, u32[]{:S(2)}) collective-permute-start(bf16[128,2048]{1,0:T(8,128)(2,1)S(1)} %collective-permute-done.3), channel_id=1, source_target_pairs={{2,0},{4,2},{6,4},{7,6},{5,7},{3,5},{1,3},{0,1},{10,8},{12,10},{14... | collective-permute-start | bytes 1572872 | tf_op jit(solution)/shard_map/ppermute | solution.py:766
  81.8 89.2 %all-to-all-start.1 = ((bf16[8,64,1536]{2,1,0:T(8,128)(2,1)}), bf16[8,64,1536]{2,1,0:T(8,128)(2,1)}, u32[]{:S(2)}, u32[]{:S(2)}) async-start(bf16[8,64,1536]{2,1,0:T(8,128)(2,1)} %shard_map.238), calls=%async_computation.1 | async-start | bytes 3145728 | tf_op jit(solution)/shard_map/all_to_all | solution.py:876
  86.2 85.1 %all-gather.9.cloned.1.call-start = ((), (), s32[]{:S(2)}) async-start(), calls=%async_computation.8 | async-start | bytes 1310720 | tf_op jit(solution)/shard_map/all_gather | solution.py:854
  87.0 33.8 %collective-permute-start.8 = (bf16[128,2048]{1,0:T(8,128)(2,1)S(1)}, bf16[128,2048]{1,0:T(8,128)(2,1)S(1)}, u32[]{:S(2)}, u32[]{:S(2)}) collective-permute-start(bf16[128,2048]{1,0:T(8,128)(2,1)S(1)} %bitcast.66), channel_id=1, source_target_pairs={{0,2},{2,4},{4,6},{6,7},{7,5},{5,3},{3,1},{1,0},{8,10},{10,12},{12... | collective-permute-start | bytes 1572872 | tf_op jit(solution)/shard_map/ppermute | solution.py:763
  88.8 36.7 %collective-permute-start.9 = (bf16[128,2048]{1,0:T(8,128)(2,1)S(1)}, bf16[128,2048]{1,0:T(8,128)(2,1)S(1)}, u32[]{:S(2)}, u32[]{:S(2)}) collective-permute-start(bf16[128,2048]{1,0:T(8,128)(2,1)S(1)} %bitcast.67), channel_id=1, source_target_pairs={{2,0},{4,2},{6,4},{7,6},{5,7},{3,5},{1,3},{0,1},{10,8},{12,10},{14... | collective-permute-start | bytes 1572872 | tf_op jit(solution)/shard_map/ppermute | solution.py:766
  89.0 18.1 %collective-permute-start.10 = (bf16[64,2048]{1,0:T(8,128)(2,1)}, bf16[64,2048]{1,0:T(8,128)(2,1)S(1)}, u32[]{:S(2)}, u32[]{:S(2)}) collective-permute-start(bf16[64,2048]{1,0:T(8,128)(2,1)} %param.20), channel_id=1, source_target_pairs={{0,0},{1,8},{2,16},{3,24},{4,4},{5,12},{6,20},{7,28},{8,1},{9,9},{... | collective-permute-start | bytes 786440 | tf_op jit(solution)/shard_map/ppermute | solution.py:885
  125.5 96.4 %all-gather.11.cloned.1.call-start = ((), (), s32[]{:S(2)}) async-start(), calls=%async_computation.9 | async-start | bytes 7864320 | tf_op jit(solution)/shard_map/all_gather | solution.py:854
  125.5 19.1 %collective-permute-start.11 = (bf16[128,2048]{1,0:T(8,128)(2,1)S(1)}, bf16[128,2048]{1,0:T(8,128)(2,1)S(1)}, u32[]{:S(2)}, u32[]{:S(2)}) collective-permute-start(bf16[128,2048]{1,0:T(8,128)(2,1)S(1)} %collective-permute-done.8.refs_2_.refs_6_), channel_id=1, source_target_pairs={{0,2},{2,4},{4,6},{6,7},{7,5},{5,3},{3,1},{1,0},{8,10},{10,12},{12... | collective-permute-start | bytes 1572872 | tf_op jit(solution)/shard_map/ppermute | solution.py:763
  132.9 14.1 %collective-permute-start.12 = (bf16[128,2048]{1,0:T(8,128)(2,1)S(1)}, bf16[128,2048]{1,0:T(8,128)(2,1)}, u32[]{:S(2)}, u32[]{:S(2)}) collective-permute-start(bf16[128,2048]{1,0:T(8,128)(2,1)S(1)} %collective-permute-done.9.refs_3_.refs_7_), channel_id=1, source_target_pairs={{2,0},{4,2},{6,4},{7,6},{5,7},{3,5},{1,3},{0,1},{10,8},{12,10},{14... | collective-permute-start | bytes 1572872 | tf_op jit(solution)/shard_map/ppermute | solution.py:766
  147.0 13.1 %collective-permute-start.13 = (bf16[128,2048]{1,0:T(8,128)(2,1)S(1)}, bf16[128,2048]{1,0:T(8,128)(2,1)S(1)}, u32[]{:S(2)}, u32[]{:S(2)}) collective-permute-start(bf16[128,2048]{1,0:T(8,128)(2,1)S(1)} %collective-permute-done.11.refs_2_.refs_8_), channel_id=1, source_target_pairs={{0,2},{2,4},{4,6},{6,7},{7,5},{5,3},{3,1},{1,0},{8,10},{10,12},{12... | collective-permute-start | bytes 1572872 | tf_op jit(solution)/shard_map/ppermute | solution.py:763
  148.4 13.5 %collective-permute-start.14 = (bf16[128,2048]{1,0:T(8,128)(2,1)}, bf16[128,2048]{1,0:T(8,128)(2,1)S(1)}, u32[]{:S(2)}, u32[]{:S(2)}) collective-permute-start(bf16[128,2048]{1,0:T(8,128)(2,1)} %collective-permute-done.12.refs_3_.refs_9_), channel_id=1, source_target_pairs={{2,0},{4,2},{6,4},{7,6},{5,7},{3,5},{1,3},{0,1},{10,8},{12,10},{14... | collective-permute-start | bytes 1572872 | tf_op jit(solution)/shard_map/ppermute | solution.py:766
  171.0 252.2 %reduce-scatter.3.cloned.1.call-start = ((), (), s32[]{:S(2)}) async-start(), calls=%async_computation.10 | async-start | bytes 7864320 | tf_op jit(solution)/shard_map/reduce_scatter | solution.py:857
  182.3 11.2 %collective-permute-start.20 = (bf16[128,2048]{1,0:T(8,128)(2,1)S(1)}, bf16[128,2048]{1,0:T(8,128)(2,1)S(1)}, u32[]{:S(2)}, u32[]{:S(2)}) collective-permute-start(bf16[128,2048]{1,0:T(8,128)(2,1)S(1)} %get-tuple-element.307), channel_id=1, source_target_pairs={{2,0},{4,2},{6,4},{7,6},{5,7},{3,5},{1,3},{0,1},{10,8},{12,10},{14... | collective-permute-start | bytes 1572872 | tf_op jit(solution)/shard_map/ppermute | solution.py:766
  219.9 13.1 %collective-permute-start.25 = (bf16[128,2048]{1,0:T(8,128)(2,1)}, bf16[128,2048]{1,0:T(8,128)(2,1)}, u32[]{:S(2)}, u32[]{:S(2)}) collective-permute-start(bf16[128,2048]{1,0:T(8,128)(2,1)} %multiply_convert_fusion.refs_0_), channel_id=1, source_target_pairs={{0,2},{2,4},{4,6},{6,7},{7,5},{5,3},{3,1},{1,0},{8,10},{10,12},{12... | collective-permute-start | bytes 1572872 | tf_op jit(solution)/shard_map/ppermute | solution.py:763
  220.3 12.7 %collective-permute-start.26 = (bf16[128,2048]{1,0:T(8,128)(2,1)}, bf16[128,2048]{1,0:T(8,128)(2,1)}, u32[]{:S(2)}, u32[]{:S(2)}) collective-permute-start(bf16[128,2048]{1,0:T(8,128)(2,1)} %multiply_convert_fusion.refs_0_), channel_id=1, source_target_pairs={{2,0},{4,2},{6,4},{7,6},{5,7},{3,5},{1,3},{0,1},{10,8},{12,10},{14... | collective-permute-start | bytes 1572872 | tf_op jit(solution)/shard_map/ppermute | solution.py:766
  233.0 13.2 %collective-permute-start.27 = (bf16[128,2048]{1,0:T(8,128)(2,1)}, bf16[128,2048]{1,0:T(8,128)(2,1)S(1)}, u32[]{:S(2)}, u32[]{:S(2)}) collective-permute-start(bf16[128,2048]{1,0:T(8,128)(2,1)} %collective-permute-done.25.refs_0_.refs_1_), channel_id=1, source_target_pairs={{0,2},{2,4},{4,6},{6,7},{7,5},{5,3},{3,1},{1,0},{8,10},{10,12},{12... | collective-permute-start | bytes 1572872 | tf_op jit(solution)/shard_map/ppermute | solution.py:763
  233.4 12.7 %collective-permute-start.28 = (bf16[128,2048]{1,0:T(8,128)(2,1)}, bf16[128,2048]{1,0:T(8,128)(2,1)S(1)}, u32[]{:S(2)}, u32[]{:S(2)}) collective-permute-start(bf16[128,2048]{1,0:T(8,128)(2,1)} %collective-permute-done.26.refs_1_.refs_2_), channel_id=1, source_target_pairs={{2,0},{4,2},{6,4},{7,6},{5,7},{3,5},{1,3},{0,1},{10,8},{12,10},{14... | collective-permute-start | bytes 1572872 | tf_op jit(solution)/shard_map/ppermute | solution.py:766
  246.1 12.0 %collective-permute-start.29 = (bf16[128,2048]{1,0:T(8,128)(2,1)S(1)}, bf16[128,2048]{1,0:T(8,128)(2,1)S(1)}, u32[]{:S(2)}, u32[]{:S(2)}) collective-permute-start(bf16[128,2048]{1,0:T(8,128)(2,1)S(1)} %collective-permute-done.27.refs_0_.refs_3_), channel_id=1, source_target_pairs={{0,2},{2,4},{4,6},{6,7},{7,5},{5,3},{3,1},{1,0},{8,10},{10,12},{12... | collective-permute-start | bytes 1572872 | tf_op jit(solution)/shard_map/ppermute | solution.py:763
  246.2 12.4 %collective-permute-start.30 = (bf16[128,2048]{1,0:T(8,128)(2,1)S(1)}, bf16[128,2048]{1,0:T(8,128)(2,1)S(1)}, u32[]{:S(2)}, u32[]{:S(2)}) collective-permute-start(bf16[128,2048]{1,0:T(8,128)(2,1)S(1)} %collective-permute-done.28.refs_1_.refs_4_), channel_id=1, source_target_pairs={{2,0},{4,2},{6,4},{7,6},{5,7},{3,5},{1,3},{0,1},{10,8},{12,10},{14... | collective-permute-start | bytes 1572872 | tf_op jit(solution)/shard_map/ppermute | solution.py:766
  273.9 12.4 %collective-permute-start.35 = (bf16[64,2048]{1,0:T(8,128)(2,1)S(1)}, bf16[64,2048]{1,0:T(8,128)(2,1)S(1)}, u32[]{:S(2)}, u32[]{:S(2)}) collective-permute-start(bf16[64,2048]{1,0:T(8,128)(2,1)S(1)} %get-tuple-element.367), channel_id=1, source_target_pairs={{0,2},{2,4},{4,6},{6,7},{7,5},{5,3},{3,1},{1,0},{8,10},{10,12},{12... | collective-permute-start | bytes 786440 | tf_op jit(solution)/shard_map/ppermute | solution.py:763
  276.9 12.6 %collective-permute-start.36 = (bf16[64,2048]{1,0:T(8,128)(2,1)S(1)}, bf16[64,2048]{1,0:T(8,128)(2,1)S(1)}, u32[]{:S(2)}, u32[]{:S(2)}) collective-permute-start(bf16[64,2048]{1,0:T(8,128)(2,1)S(1)} %get-tuple-element.368), channel_id=1, source_target_pairs={{2,0},{4,2},{6,4},{7,6},{5,7},{3,5},{1,3},{0,1},{10,8},{12,10},{14... | collective-permute-start | bytes 786440 | tf_op jit(solution)/shard_map/ppermute | solution.py:766
  289.8 17.1 %collective-permute-start.37 = (bf16[128,2048]{1,0:T(8,128)(2,1)S(1)}, bf16[128,2048]{1,0:T(8,128)(2,1)}, u32[]{:S(2)}, u32[]{:S(2)}) collective-permute-start(bf16[128,2048]{1,0:T(8,128)(2,1)S(1)} %get-tuple-element.379), channel_id=1, source_target_pairs={{0,2},{2,4},{4,6},{6,7},{7,5},{5,3},{3,1},{1,0},{8,10},{10,12},{12... | collective-permute-start | bytes 1572872 | tf_op jit(solution)/shard_map/ppermute | solution.py:763
  292.0 14.9 %collective-permute-start.38 = (bf16[128,2048]{1,0:T(8,128)(2,1)S(1)}, bf16[128,2048]{1,0:T(8,128)(2,1)}, u32[]{:S(2)}, u32[]{:S(2)}) collective-permute-start(bf16[128,2048]{1,0:T(8,128)(2,1)S(1)} %get-tuple-element.380), channel_id=1, source_target_pairs={{2,0},{4,2},{6,4},{7,6},{5,7},{3,5},{1,3},{0,1},{10,8},{12,10},{14... | collective-permute-start | bytes 1572872 | tf_op jit(solution)/shard_map/ppermute | solution.py:766
  292.0 15.2 %collective-permute-start.39 = (bf16[128,2048]{1,0:T(8,128)(2,1)S(1)}, bf16[128,2048]{1,0:T(8,128)(2,1)}, u32[]{:S(2)}, u32[]{:S(2)}) collective-permute-start(bf16[128,2048]{1,0:T(8,128)(2,1)S(1)} %get-tuple-element.381), channel_id=1, source_target_pairs={{0,2},{2,4},{4,6},{6,7},{7,5},{5,3},{3,1},{1,0},{8,10},{10,12},{12... | collective-permute-start | bytes 1572872 | tf_op jit(solution)/shard_map/ppermute | solution.py:763
  294.0 16.0 %collective-permute-start.40 = (bf16[128,2048]{1,0:T(8,128)(2,1)S(1)}, bf16[128,2048]{1,0:T(8,128)(2,1)}, u32[]{:S(2)}, u32[]{:S(2)}) collective-permute-start(bf16[128,2048]{1,0:T(8,128)(2,1)S(1)} %get-tuple-element.382), channel_id=1, source_target_pairs={{2,0},{4,2},{6,4},{7,6},{5,7},{3,5},{1,3},{0,1},{10,8},{12,10},{14... | collective-permute-start | bytes 1572872 | tf_op jit(solution)/shard_map/ppermute | solution.py:766
  315.7 12.3 %collective-permute-start.41 = (bf16[128,2048]{1,0:T(8,128)(2,1)}, bf16[128,2048]{1,0:T(8,128)(2,1)S(1)}, u32[]{:S(2)}, u32[]{:S(2)}) collective-permute-start(bf16[128,2048]{1,0:T(8,128)(2,1)} %get-tuple-element.398), channel_id=1, source_target_pairs={{0,2},{2,4},{4,6},{6,7},{7,5},{5,3},{3,1},{1,0},{8,10},{10,12},{12... | collective-permute-start | bytes 1572872 | tf_op jit(solution)/shard_map/ppermute | solution.py:763
  318.2 12.5 %collective-permute-start.42 = (bf16[128,2048]{1,0:T(8,128)(2,1)}, bf16[128,2048]{1,0:T(8,128)(2,1)S(1)}, u32[]{:S(2)}, u32[]{:S(2)}) collective-permute-start(bf16[128,2048]{1,0:T(8,128)(2,1)} %get-tuple-element.399), channel_id=1, source_target_pairs={{2,0},{4,2},{6,4},{7,6},{5,7},{3,5},{1,3},{0,1},{10,8},{12,10},{14... | collective-permute-start | bytes 1572872 | tf_op jit(solution)/shard_map/ppermute | solution.py:766
  318.2 21.0 %collective-permute-start.43 = (bf16[128,2048]{1,0:T(8,128)(2,1)}, bf16[128,2048]{1,0:T(8,128)(2,1)}, u32[]{:S(2)}, u32[]{:S(2)}) collective-permute-start(bf16[128,2048]{1,0:T(8,128)(2,1)} %get-tuple-element.400), channel_id=1, source_target_pairs={{0,2},{2,4},{4,6},{6,7},{7,5},{5,3},{3,1},{1,0},{8,10},{10,12},{12... | collective-permute-start | bytes 1572872 | tf_op jit(solution)/shard_map/ppermute | solution.py:763
  320.2 21.8 %collective-permute-start.44 = (bf16[128,2048]{1,0:T(8,128)(2,1)}, bf16[128,2048]{1,0:T(8,128)(2,1)}, u32[]{:S(2)}, u32[]{:S(2)}) collective-permute-start(bf16[128,2048]{1,0:T(8,128)(2,1)} %get-tuple-element.401), channel_id=1, source_target_pairs={{2,0},{4,2},{6,4},{7,6},{5,7},{3,5},{1,3},{0,1},{10,8},{12,10},{14... | collective-permute-start | bytes 1572872 | tf_op jit(solution)/shard_map/ppermute | solution.py:766
  344.0 12.7 %collective-permute-start.45 = (bf16[128,2048]{1,0:T(8,128)(2,1)S(1)}, bf16[128,2048]{1,0:T(8,128)(2,1)S(1)}, u32[]{:S(2)}, u32[]{:S(2)}) collective-permute-start(bf16[128,2048]{1,0:T(8,128)(2,1)S(1)} %get-tuple-element.406), channel_id=1, source_target_pairs={{0,2},{2,4},{4,6},{6,7},{7,5},{5,3},{3,1},{1,0},{8,10},{10,12},{12... | collective-permute-start | bytes 1572872 | tf_op jit(solution)/shard_map/ppermute | solution.py:763
  344.8 12.9 %collective-permute-start.46 = (bf16[128,2048]{1,0:T(8,128)(2,1)S(1)}, bf16[128,2048]{1,0:T(8,128)(2,1)S(1)}, u32[]{:S(2)}, u32[]{:S(2)}) collective-permute-start(bf16[128,2048]{1,0:T(8,128)(2,1)S(1)} %get-tuple-element.407), channel_id=1, source_target_pairs={{2,0},{4,2},{6,4},{7,6},{5,7},{3,5},{1,3},{0,1},{10,8},{12,10},{14... | collective-permute-start | bytes 1572872 | tf_op jit(solution)/shard_map/ppermute | solution.py:766
  346.1 18.4 %collective-permute-start.47 = (bf16[128,2048]{1,0:T(8,128)(2,1)S(1)}, bf16[128,2048]{1,0:T(8,128)(2,1)S(1)}, u32[]{:S(2)}, u32[]{:S(2)}) collective-permute-start(bf16[128,2048]{1,0:T(8,128)(2,1)S(1)} %get-tuple-element.408), channel_id=1, source_target_pairs={{0,2},{2,4},{4,6},{6,7},{7,5},{5,3},{3,1},{1,0},{8,10},{10,12},{12... | collective-permute-start | bytes 1572872 | tf_op jit(solution)/shard_map/ppermute | solution.py:763
  346.8 18.4 %collective-permute-start.48 = (bf16[128,2048]{1,0:T(8,128)(2,1)S(1)}, bf16[128,2048]{1,0:T(8,128)(2,1)S(1)}, u32[]{:S(2)}, u32[]{:S(2)}) collective-permute-start(bf16[128,2048]{1,0:T(8,128)(2,1)S(1)} %get-tuple-element.409), channel_id=1, source_target_pairs={{2,0},{4,2},{6,4},{7,6},{5,7},{3,5},{1,3},{0,1},{10,8},{12,10},{14... | collective-permute-start | bytes 1572872 | tf_op jit(solution)/shard_map/ppermute | solution.py:766
  367.7 12.3 %collective-permute-start.49 = (bf16[128,2048]{1,0:T(8,128)(2,1)S(1)}, bf16[128,2048]{1,0:T(8,128)(2,1)S(1)}, u32[]{:S(2)}, u32[]{:S(2)}) collective-permute-start(bf16[128,2048]{1,0:T(8,128)(2,1)S(1)} %get-tuple-element.446.refs_9_), channel_id=1, source_target_pairs={{0,2},{2,4},{4,6},{6,7},{7,5},{5,3},{3,1},{1,0},{8,10},{10,12},{12... | collective-permute-start | bytes 1572872 | tf_op jit(solution)/shard_map/ppermute | solution.py:763
  367.8 12.3 %collective-permute-start.50 = (bf16[128,2048]{1,0:T(8,128)(2,1)S(1)}, bf16[128,2048]{1,0:T(8,128)(2,1)S(1)}, u32[]{:S(2)}, u32[]{:S(2)}) collective-permute-start(bf16[128,2048]{1,0:T(8,128)(2,1)S(1)} %get-tuple-element.446.refs_9_), channel_id=1, source_target_pairs={{2,0},{4,2},{6,4},{7,6},{5,7},{3,5},{1,3},{0,1},{10,8},{12,10},{14... | collective-permute-start | bytes 1572872 | tf_op jit(solution)/shard_map/ppermute | solution.py:766
  369.9 13.4 %collective-permute-start.58 = (bf16[192,2048]{1,0:T(8,128)(2,1)S(1)}, bf16[192,2048]{1,0:T(8,128)(2,1)S(1)}, u32[]{:S(2)}, u32[]{:S(2)}) collective-permute-start(bf16[192,2048]{1,0:T(8,128)(2,1)S(1)} %get-tuple-element.500), channel_id=1, source_target_pairs={{0,8},{8,0},{16,24},{24,16},{1,9},{9,1},{17,25},{25,17},{2,10},{10... | collective-permute-start | bytes 2359304 | tf_op jit(solution)/shard_map/ppermute | solution.py:860
  370.0 39.1 %collective-permute-start.57 = (bf16[192,2048]{1,0:T(8,128)(2,1)S(1)}, bf16[192,2048]{1,0:T(8,128)(2,1)S(1)}, u32[]{:S(2)}, u32[]{:S(2)}) collective-permute-start(bf16[192,2048]{1,0:T(8,128)(2,1)S(1)} %get-tuple-element.499), channel_id=1, source_target_pairs={{0,8},{8,0},{16,24},{24,16},{1,9},{9,1},{17,25},{25,17},{2,10},{10... | collective-permute-start | bytes 2359304 | tf_op jit(solution)/shard_map/ppermute | solution.py:860
  380.1 13.6 %collective-permute-start.51 = (bf16[128,2048]{1,0:T(8,128)(2,1)S(1)}, bf16[128,2048]{1,0:T(8,128)(2,1)S(1)}, u32[]{:S(2)}, u32[]{:S(2)}) collective-permute-start(bf16[128,2048]{1,0:T(8,128)(2,1)S(1)} %collective-permute-done.49.refs_10_), channel_id=1, source_target_pairs={{0,2},{2,4},{4,6},{6,7},{7,5},{5,3},{3,1},{1,0},{8,10},{10,12},{12... | collective-permute-start | bytes 1572872 | tf_op jit(solution)/shard_map/ppermute | solution.py:763
  380.1 13.6 %collective-permute-start.52 = (bf16[128,2048]{1,0:T(8,128)(2,1)S(1)}, bf16[128,2048]{1,0:T(8,128)(2,1)S(1)}, u32[]{:S(2)}, u32[]{:S(2)}) collective-permute-start(bf16[128,2048]{1,0:T(8,128)(2,1)S(1)} %collective-permute-done.50.refs_11_), channel_id=1, source_target_pairs={{2,0},{4,2},{6,4},{7,6},{5,7},{3,5},{1,3},{0,1},{10,8},{12,10},{14... | collective-permute-start | bytes 1572872 | tf_op jit(solution)/shard_map/ppermute | solution.py:766
  383.6 25.5 %collective-permute-start.59 = (bf16[192,2048]{1,0:T(8,128)(2,1)S(1)}, bf16[192,2048]{1,0:T(8,128)(2,1)S(1)}, u32[]{:S(2)}, u32[]{:S(2)}) collective-permute-start(bf16[192,2048]{1,0:T(8,128)(2,1)S(1)} %add_convert_fusion), channel_id=1, source_target_pairs={{0,16},{8,24},{16,0},{24,8},{1,17},{9,25},{17,1},{25,9},{2,18},{10... | collective-permute-start | bytes 2359304 | tf_op jit(solution)/shard_map/ppermute | solution.py:860
  393.7 12.4 %collective-permute-start.53 = (bf16[128,2048]{1,0:T(8,128)(2,1)S(1)}, bf16[128,2048]{1,0:T(8,128)(2,1)S(1)}, u32[]{:S(2)}, u32[]{:S(2)}) collective-permute-start(bf16[128,2048]{1,0:T(8,128)(2,1)S(1)} %collective-permute-done.51.refs_12_), channel_id=1, source_target_pairs={{0,2},{2,4},{4,6},{6,7},{7,5},{5,3},{3,1},{1,0},{8,10},{10,12},{12... | collective-permute-start | bytes 1572872 | tf_op jit(solution)/shard_map/ppermute | solution.py:763
  393.7 12.3 %collective-permute-start.54 = (bf16[128,2048]{1,0:T(8,128)(2,1)S(1)}, bf16[128,2048]{1,0:T(8,128)(2,1)S(1)}, u32[]{:S(2)}, u32[]{:S(2)}) collective-permute-start(bf16[128,2048]{1,0:T(8,128)(2,1)S(1)} %collective-permute-done.52.refs_13_), channel_id=1, source_target_pairs={{2,0},{4,2},{6,4},{7,6},{5,7},{3,5},{1,3},{0,1},{10,8},{12,10},{14... | collective-permute-start | bytes 1572872 | tf_op jit(solution)/shard_map/ppermute | solution.py:766
  423.2 36.7 %all-to-all-start.2 = ((bf16[8,64,1536]{2,1,0:T(8,128)(2,1)}), bf16[8,64,1536]{2,1,0:T(8,128)(2,1)}, u32[]{:S(2)}, u32[]{:S(2)}) async-start(bf16[8,64,1536]{2,1,0:T(8,128)(2,1)} %bitcast.77), calls=%async_computation.3 | async-start | bytes 3145728 | tf_op jit(solution)/shard_map/all_to_all | solution.py:876
  429.8 58.5 %reduce-scatter.5.cloned.1.call-start = ((), (), s32[]{:S(2)}) async-start(), calls=%async_computation.11 | async-start | bytes 1310720 | tf_op jit(solution)/shard_map/reduce_scatter | solution.py:857
  442.0 17.9 %collective-permute-start.60 = (bf16[64,2048]{1,0:T(8,128)(2,1)}, bf16[64,2048]{1,0:T(8,128)(2,1)}, u32[]{:S(2)}, u32[]{:S(2)}) collective-permute-start(bf16[64,2048]{1,0:T(8,128)(2,1)} %get-tuple-element.441), channel_id=1, source_target_pairs={{0,2},{2,4},{4,6},{6,7},{7,5},{5,3},{3,1},{1,0},{8,10},{10,12},{12... | collective-permute-start | bytes 786440 | tf_op jit(solution)/shard_map/ppermute | solution.py:763
  444.1 15.9 %collective-permute-start.61 = (bf16[64,2048]{1,0:T(8,128)(2,1)}, bf16[64,2048]{1,0:T(8,128)(2,1)}, u32[]{:S(2)}, u32[]{:S(2)}) collective-permute-start(bf16[64,2048]{1,0:T(8,128)(2,1)} %get-tuple-element.442), channel_id=1, source_target_pairs={{2,0},{4,2},{6,4},{7,6},{5,7},{3,5},{1,3},{0,1},{10,8},{12,10},{14... | collective-permute-start | bytes 786440 | tf_op jit(solution)/shard_map/ppermute | solution.py:766
  444.1 21.6 %collective-permute-start.68 = (bf16[640,512]{1,0:T(8,128)(2,1)}, bf16[640,512]{1,0:T(8,128)(2,1)S(1)}, u32[]{:S(2)}, u32[]{:S(2)}) collective-permute-start(bf16[640,512]{1,0:T(8,128)(2,1)} %get-tuple-element.501), channel_id=1, source_target_pairs={{0,8},{8,0},{16,24},{24,16},{1,9},{9,1},{17,25},{25,17},{2,10},{10... | collective-permute-start | bytes 1966088 | tf_op jit(solution)/shard_map/ppermute | solution.py:860
  451.4 20.4 %collective-permute-start.70 = (bf16[640,512]{1,0:T(8,128)(2,1)S(1)}, bf16[640,512]{1,0:T(8,128)(2,1)S(1)}, u32[]{:S(2)}, u32[]{:S(2)}) collective-permute-start(bf16[640,512]{1,0:T(8,128)(2,1)S(1)} %add_convert_fusion.2), channel_id=1, source_target_pairs={{0,16},{8,24},{16,0},{24,8},{1,17},{9,25},{17,1},{25,9},{2,18},{10... | collective-permute-start | bytes 1966088 | tf_op jit(solution)/shard_map/ppermute | solution.py:860
  462.3 21.1 %collective-permute-start.62 = (bf16[128,2048]{1,0:T(8,128)(2,1)}, bf16[128,2048]{1,0:T(8,128)(2,1)}, u32[]{:S(2)}, u32[]{:S(2)}) collective-permute-start(bf16[128,2048]{1,0:T(8,128)(2,1)} %get-tuple-element.460), channel_id=1, source_target_pairs={{0,2},{2,4},{4,6},{6,7},{7,5},{5,3},{3,1},{1,0},{8,10},{10,12},{12... | collective-permute-start | bytes 1572872 | tf_op jit(solution)/shard_map/ppermute | solution.py:763
  465.8 17.6 %collective-permute-start.63 = (bf16[128,2048]{1,0:T(8,128)(2,1)S(1)}, bf16[128,2048]{1,0:T(8,128)(2,1)}, u32[]{:S(2)}, u32[]{:S(2)}) collective-permute-start(bf16[128,2048]{1,0:T(8,128)(2,1)S(1)} %get-tuple-element.461), channel_id=1, source_target_pairs={{2,0},{4,2},{6,4},{7,6},{5,7},{3,5},{1,3},{0,1},{10,8},{12,10},{14... | collective-permute-start | bytes 1572872 | tf_op jit(solution)/shard_map/ppermute | solution.py:766
  474.0 39.6 %all-to-all-start.3 = ((bf16[8,80,512]{2,1,0:T(8,128)(2,1)}), bf16[8,80,512]{2,1,0:T(8,128)(2,1)S(1)}, u32[]{:S(2)}, u32[]{:S(2)}) async-start(bf16[8,80,512]{2,1,0:T(8,128)(2,1)} %bitcast.13), calls=%async_computation.4 | async-start | bytes 1310720 | tf_op jit(solution)/shard_map/all_to_all | solution.py:876
  486.2 16.1 %collective-permute-start.64 = (bf16[128,2048]{1,0:T(8,128)(2,1)}, bf16[128,2048]{1,0:T(8,128)(2,1)S(1)}, u32[]{:S(2)}, u32[]{:S(2)}) collective-permute-start(bf16[128,2048]{1,0:T(8,128)(2,1)} %get-tuple-element.467), channel_id=1, source_target_pairs={{0,2},{2,4},{4,6},{6,7},{7,5},{5,3},{3,1},{1,0},{8,10},{10,12},{12... | collective-permute-start | bytes 1572872 | tf_op jit(solution)/shard_map/ppermute | solution.py:763
  488.3 17.7 %collective-permute-start.65 = (bf16[128,2048]{1,0:T(8,128)(2,1)S(1)}, bf16[128,2048]{1,0:T(8,128)(2,1)}, u32[]{:S(2)}, u32[]{:S(2)}) collective-permute-start(bf16[128,2048]{1,0:T(8,128)(2,1)S(1)} %get-tuple-element.468), channel_id=1, source_target_pairs={{2,0},{4,2},{6,4},{7,6},{5,7},{3,5},{1,3},{0,1},{10,8},{12,10},{14... | collective-permute-start | bytes 1572872 | tf_op jit(solution)/shard_map/ppermute | solution.py:766
  488.3 24.5 %collective-permute-start.71 = (bf16[64,2048]{1,0:T(8,128)(2,1)}, bf16[64,2048]{1,0:T(8,128)(2,1)S(1)}, u32[]{:S(2)}, u32[]{:S(2)}) collective-permute-start(bf16[64,2048]{1,0:T(8,128)(2,1)} %reduce-scatter.5.cloned.1.call-done), channel_id=1, source_target_pairs={{0,0},{8,1},{16,2},{24,3},{4,4},{12,5},{20,6},{28,7},{1,8},{9,9},{... | collective-permute-start | bytes 786440 | tf_op jit(solution)/shard_map/ppermute | solution.py:885
  508.8 13.8 %collective-permute-start.66 = (bf16[128,2048]{1,0:T(8,128)(2,1)}, bf16[128,2048]{1,0:T(8,128)(2,1)S(1)}, u32[]{:S(2)}, u32[]{:S(2)}) collective-permute-start(bf16[128,2048]{1,0:T(8,128)(2,1)} %get-tuple-element.471), channel_id=1, source_target_pairs={{0,2},{2,4},{4,6},{6,7},{7,5},{5,3},{3,1},{1,0},{8,10},{10,12},{12... | collective-permute-start | bytes 1572872 | tf_op jit(solution)/shard_map/ppermute | solution.py:763
  512.1 12.6 %collective-permute-start.67 = (bf16[128,2048]{1,0:T(8,128)(2,1)}, bf16[128,2048]{1,0:T(8,128)(2,1)S(1)}, u32[]{:S(2)}, u32[]{:S(2)}) collective-permute-start(bf16[128,2048]{1,0:T(8,128)(2,1)} %get-tuple-element.472), channel_id=1, source_target_pairs={{2,0},{4,2},{6,4},{7,6},{5,7},{3,5},{1,3},{0,1},{10,8},{12,10},{14... | collective-permute-start | bytes 1572872 | tf_op jit(solution)/shard_map/ppermute | solution.py:766
  (98 other events, 1098.8 us)
Sparse Core Ops, SparseCore 0:
  52.6 28.1 all-gather.4
  82.4 28.5 all-gather.6
  125.6 21.9 all-gather.8
  171.1 43.5 all-gather.10
  310.2 60.1 reduce-scatter.2
  450.1 29.7 reduce-scatter.4
